TPU v7x, 128 devices: a whole 4x4x4 slice. The times are simulated.
128 devices in a mesh: gx: 8 (over z_lo, y), gy: 16 (over x, z_hi, core).
Axes of the slice: x: 4, y: 4, z: 4 (z_hi: 2, z_lo: 2; z = z_hi * 2 + z_lo), core: 2. Of those that a mesh axis runs over, the one named last changes fastest.
Arguments:
- velocity_now: float32 [3, 64, 256, 512], P(None, 'gx', 'gy'), may hold values from -6 to 6
- advecting: float32 [3, 64, 256, 512], P(None, 'gx', 'gy'), may hold values from -6 to 6
- cotangent: float32 [3, 64, 256, 512], P(None, 'gx', 'gy'), may hold values from -6 to 6
- building_height: int32 [64, 256], P('gx', 'gy'), may hold values from 0 to 127
- section_index: int32 [1], replicated, may hold values from 0 to 191
- vertical_modes: float32 [512, 512], replicated, may hold values from -0.25 to 0.25
- vertical_tilt: float32 [512, 512], replicated, may hold values from -0.25 to 0.25
- mode_rates: float32 [512], replicated, may hold values from 0.01 to 1
Outputs:
- velocity_next: float32 [3, 64, 256, 512], P(None, 'gx', 'gy')
- velocity_adjoint: float32 [3, 64, 256, 512], P(None, 'gx', 'gy')
All inputs are finite; a program needn't handle non-finite values.
Results may differ from a plain program's by a relative error of at most 0.000055.
Values sent between devices are 32-bit elements; how exact they have to be, the bound alone decides.
A program may use at most 192 MiB of HBM per device.

v0:
```python
import math

import jax
import jax.numpy as jnp
from jax import lax
from jax.sharding import PartitionSpec as P

stencil_taps = ((2, -1.0, 1.0), (1, 8.0, -4.0), (0, 0.0, 6.0), (-1, -8.0, -4.0), (-2, 1.0, 1.0))
highest = lax.Precision.HIGHEST


def extended(block, sides, width):
    for axis, dim in sides:
        count = lax.axis_size(axis)
        forward = [(i, i + 1) for i in range(count - 1)]
        forward.append((count - 1, 0))
        backward = [(target, source) for source, target in forward]
        low = lax.ppermute(
            lax.slice_in_dim(block, block.shape[dim] - width, None, axis=dim), axis, forward
        )
        high = lax.ppermute(lax.slice_in_dim(block, 0, width, axis=dim), axis, backward)
        block = jnp.concatenate([low, block, high], axis=dim)
    return block


def section_factor(section_index):
    section = section_index[0] % 3
    step_number = section_index[0] // 3
    step_size = jnp.float32(0.2) + jnp.float32(0.2) * step_number.astype(jnp.float32) / jnp.float32(
        63.0
    )
    fraction = jnp.where(
        section == 0,
        jnp.float32(1.0 / 3.0),
        jnp.where(section == 1, jnp.float32(0.5), jnp.float32(1.0)),
    )
    return step_size * fraction


def shifted(padded, dimension, offset, length):
    return lax.slice_in_dim(padded, 2 + offset, 2 + offset + length, axis=dimension)


def upwind(viewer, advect_speed):
    central = 0.0
    hyper_sum = 0.0
    for offset, central_weight, hyper_weight in stencil_taps:
        sample = viewer(offset)
        central = central + central_weight * sample
        hyper_sum = hyper_sum + hyper_weight * sample
    return advect_speed * central + jnp.abs(advect_speed) * hyper_sum


def pulled(weighted_view, magnitude_view):
    summed = 0.0
    for offset, central_weight, hyper_weight in stencil_taps:
        summed = (
            summed
            + central_weight * weighted_view(-offset)
            + hyper_weight * magnitude_view(-offset)
        )
    return -summed / 12.0


def scattered(weighted, magnitude, dimension):
    summed = 0.0
    for offset, central_weight, hyper_weight in stencil_taps:
        widths = [(0, 0)] * weighted.ndim
        widths[dimension] = (2 + offset, 2 - offset)
        summed = summed + jnp.pad(central_weight * weighted + hyper_weight * magnitude, widths)
    return -summed / 12.0


def tendency(padded, advecting):
    cells_x, cells_y, levels = (advecting.shape[1], advecting.shape[2], advecting.shape[3])
    rows_x = padded[:, :, 2 : 2 + cells_y]
    rows_y = padded[:, 2 : 2 + cells_x]
    column = jnp.pad(rows_y[:, :, 2 : 2 + cells_y], ((0, 0), (0, 0), (0, 0), (2, 2)))
    summed = upwind(lambda offset: shifted(rows_x, 1, offset, cells_x), advecting[0][None])
    summed = summed + upwind(lambda offset: shifted(rows_y, 2, offset, cells_y), advecting[1][None])
    summed = summed + upwind(lambda offset: shifted(column, 3, offset, levels), advecting[2][None])
    return -summed / 12.0


def full_tables(count):
    freq_index = lax.broadcasted_iota(jnp.int32, (count, count), 0)
    place = lax.broadcasted_iota(jnp.int32, (count, count), 1)
    angle = (freq_index * place % count).astype(jnp.float32) * (2.0 * math.pi / count)
    return (jnp.cos(angle), jnp.sin(angle))


def along_x(table, planes):
    return jnp.einsum("kx,bxy->bky", table, planes, precision=highest)


def along_y(planes, table):
    return jnp.einsum("bky,yl->bkl", planes, table, precision=highest)


def project(fields, vertical_modes, vertical_tilt, mode_rates):
    groups, cells_x, cells_y, levels = (
        fields.shape[0],
        fields.shape[2],
        fields.shape[3],
        fields.shape[4],
    )
    parts_x = lax.axis_size("gx")
    parts_y = lax.axis_size("gy")
    grid_x = cells_x * parts_x
    grid_y = cells_y * parts_y
    mode_count = levels // (parts_x * parts_y)
    matrices = jnp.stack([vertical_modes, vertical_modes, vertical_tilt])
    modal_data = jnp.einsum("gcxyz,czm->gcmxy", fields, matrices, precision=highest)
    flattened = modal_data.reshape(groups, 3, levels, cells_x * cells_y)
    spectral_in = lax.all_to_all(
        lax.all_to_all(flattened, "gy", split_axis=2, concat_axis=3, tiled=True),
        "gx",
        split_axis=2,
        concat_axis=3,
        tiled=True,
    )
    mode_start = lax.axis_index("gy") * (levels // parts_y) + lax.axis_index("gx") * mode_count
    blocks = spectral_in.reshape(groups * 3 * mode_count, parts_x, parts_y, cells_x, cells_y)
    planes = blocks.transpose(0, 1, 3, 2, 4).reshape(groups * 3 * mode_count, grid_x, grid_y)
    cos_x, sin_x = full_tables(grid_x)
    cos_y, sin_y = full_tables(grid_y)
    half_r = along_x(cos_x, planes)
    half_i = -along_x(sin_x, planes)
    spec_r = along_y(half_r, cos_y) + along_y(half_i, sin_y)
    spec_i = along_y(half_i, cos_y) - along_y(half_r, sin_y)
    spec_r = spec_r.reshape(groups, 3, mode_count, grid_x, grid_y)
    spec_i = spec_i.reshape(groups, 3, mode_count, grid_x, grid_y)
    angle_x = lax.broadcasted_iota(jnp.int32, (grid_x, 1), 0).astype(jnp.float32) * (
        2.0 * math.pi / grid_x
    )
    angle_y = lax.broadcasted_iota(jnp.int32, (1, grid_y), 1).astype(jnp.float32) * (
        2.0 * math.pi / grid_y
    )
    diff_xr = 1.0 - jnp.cos(angle_x)
    diff_xi = jnp.sin(angle_x)
    diff_yr = 1.0 - jnp.cos(angle_y)
    diff_yi = jnp.sin(angle_y)
    local_rates = lax.dynamic_slice_in_dim(mode_rates, mode_start, mode_count)[None, :, None, None]
    denominator = (
        local_rates
        + (diff_xr * diff_xr + diff_xi * diff_xi)
        + (diff_yr * diff_yr + diff_yi * diff_yi)
    )
    div_r = (
        diff_xr * spec_r[:, 0]
        - diff_xi * spec_i[:, 0]
        + diff_yr * spec_r[:, 1]
        - diff_yi * spec_i[:, 1]
        + spec_r[:, 2]
    )
    div_i = (
        diff_xr * spec_i[:, 0]
        + diff_xi * spec_r[:, 0]
        + diff_yr * spec_i[:, 1]
        + diff_yi * spec_r[:, 1]
        + spec_i[:, 2]
    )
    phi_r = div_r / denominator
    phi_i = div_i / denominator
    psi_r = jnp.stack(
        [diff_xr * phi_r + diff_xi * phi_i, diff_yr * phi_r + diff_yi * phi_i, phi_r], 1
    )
    psi_i = jnp.stack(
        [diff_xr * phi_i - diff_xi * phi_r, diff_yr * phi_i - diff_yi * phi_r, phi_i], 1
    )
    psi_r = psi_r.reshape(groups * 3 * mode_count, grid_x, grid_y)
    psi_i = psi_i.reshape(groups * 3 * mode_count, grid_x, grid_y)
    back_r = along_y(psi_r, cos_y) - along_y(psi_i, sin_y)
    back_i = along_y(psi_i, cos_y) + along_y(psi_r, sin_y)
    physical = along_x(cos_x, back_r) - along_x(sin_x, back_i)
    physical = physical / (grid_x * grid_y)
    regrouped = physical.reshape(
        groups * 3 * mode_count, parts_x, cells_x, parts_y, cells_y
    ).transpose(0, 1, 3, 2, 4)
    flattened_back = regrouped.reshape(groups, 3, mode_count, grid_x * grid_y)
    home_in = lax.all_to_all(
        lax.all_to_all(flattened_back, "gx", split_axis=3, concat_axis=2, tiled=True),
        "gy",
        split_axis=3,
        concat_axis=2,
        tiled=True,
    )
    home_modes = home_in.reshape(groups, 3, levels, cells_x, cells_y)
    correction = jnp.einsum("gcmxy,czm->gcxyz", home_modes, matrices, precision=highest)
    return fields - correction


def per_device(
    velocity_now,
    advecting,
    cotangent,
    building_height,
    section_index,
    vertical_modes,
    vertical_tilt,
    mode_rates,
):
    cells_x, cells_y, levels = (velocity_now.shape[1], velocity_now.shape[2], velocity_now.shape[3])
    level_index = lax.broadcasted_iota(jnp.int32, (cells_x, cells_y, levels), 2)
    fluid_cells = (level_index >= building_height[:, :, None]).astype(jnp.float32)
    factor = section_factor(section_index)

    def project_all(fields):
        return project(fields, vertical_modes, vertical_tilt, mode_rates)

    padded = extended(velocity_now, (("gx", 1), ("gy", 2)), 2)
    section_value = fluid_cells * (velocity_now + factor * tendency(padded, advecting))
    projected = project_all(cotangent[None])[0]
    velocity_next = project_all(section_value[None])[0]
    gradient = fluid_cells * projected
    speed_z = advecting[2][None]
    level_pads = ((0, 0), (0, 0), (0, 0), (2, 2))
    weighted_z = jnp.pad(speed_z * gradient, level_pads)
    magnitude_z = jnp.pad(jnp.abs(speed_z) * gradient, level_pads)
    inner_z = pulled(
        lambda offset: shifted(weighted_z, 3, offset, levels),
        lambda offset: shifted(magnitude_z, 3, offset, levels),
    )
    speed_x = advecting[0][None]
    summed_x = scattered(speed_x * gradient, jnp.abs(speed_x) * gradient, 1)
    edges_x = jnp.concatenate([summed_x[:, 0:2], summed_x[:, cells_x + 2 :]], 1)
    arrived_x = extended(edges_x, (("gx", 1),), 2)
    inner_x = summed_x[:, 2 : cells_x + 2]
    inner_x = inner_x.at[:, 0:2].add(arrived_x[:, 0:2]).at[:, cells_x - 2 :].add(arrived_x[:, 6:8])
    speed_y = advecting[1][None]
    summed_y = scattered(speed_y * gradient, jnp.abs(speed_y) * gradient, 2)
    edges_y = jnp.concatenate([summed_y[:, :, 0:2], summed_y[:, :, cells_y + 2 :]], 2)
    arrived_y = extended(edges_y, (("gy", 2),), 2)
    inner_y = summed_y[:, :, 2 : cells_y + 2]
    inner_y = (
        inner_y.at[:, :, 0:2]
        .add(arrived_y[:, :, 0:2])
        .at[:, :, cells_y - 2 :]
        .add(arrived_y[:, :, 6:8])
    )
    velocity_adjoint = gradient + factor * (inner_x + inner_y + inner_z)
    return (velocity_next, velocity_adjoint)


def solution(mesh):
    in_specs = (
        P(None, "gx", "gy", None),
        P(None, "gx", "gy", None),
        P(None, "gx", "gy", None),
        P("gx", "gy"),
        P(),
        P(),
        P(),
        P(),
    )
    out_specs = (P(None, "gx", "gy", None), P(None, "gx", "gy", None))
    return jax.shard_map(
        per_device, mesh=mesh, in_specs=in_specs, out_specs=out_specs, check_vma=False
    )
```

profile of v0, /device:TPU:1, one launch (start us, length us, event | category | flops | bytes accessed | tf_op | source)
XLA Modules:
  0.0 840.8 jit_solution(14105554571285261599)
XLA Ops:
  12.4 8.3 all-to-all-start.4
  40.4 7.1 all-to-all-start
  49.0 12.7 %all-to-all-done = f32[1,3,512,128]{3,0,1,2:T(1,128)S(1)} async-done(((f32[1,3,512,128]{3,0,1,2:T(1,128)}), f32[1,3,512,128]{3,0,1,2:T(1,128)S(1)}, u32[]{:S(2)}, u32[]{:S(2)}) %all-to-all-start) | async-done | bytes 786464 | tf_op jit(solution)/shard_map/all_to_all | solution.py:116
  68.7 10.5 %all-to-all-done.5 = f32[1,3,32,2048]{3,0,1,2:T(1,128)S(1)} async-done(((f32[1,3,32,2048]{3,0,1,2:T(1,128)}), f32[1,3,32,2048]{3,0,1,2:T(1,128)S(1)}, u32[]{:S(2)}, u32[]{:S(2)}) %all-to-all-start.5) | async-done | bytes 786464 | tf_op jit(solution)/shard_map/all_to_all | solution.py:115
  87.7 6.9 copy.120
  113.1 6.9 copy.106
  154.5 8.4 %copy.132 = f32[12,8,8,16,16]{4,2,3,1,0:T(8,128)} copy(f32[12,8,8,16,16]{4,3,2,1,0:T(8,128)} %reshape.511) | data formatting | bytes 1572864 | tf_op jit(solution)/shard_map/reshape | solution.py:177
  168.3 37.1 %copy.108 = f32[1,3,4,16384]{2,0,1,3:T(1,128)} copy(f32[1,3,4,16384]{3,2,1,0:T(4,128)S(1)} %reshape.512) | data formatting | bytes 1572864 | tf_op jit(solution)/shard_map/reshape | solution.py:180
  206.0 86.9 %reduce.8 = f32[16384,3,4]{2,1,0:T(4,128)} reduce(f32[16384,3,1,4]{3,2,1,0:T(1,128)} %bitcast.210, f32[]{:T(128)} %broadcast.766), dimensions={2}, to_apply=%bitcast.170.reduce_sub_computation | reduce | bytes 1572868
  292.9 21.0 %reshape.534 = f32[8,1,24576]{2,1,0:T(1,128)} reshape(f32[16384,3,4]{2,1,0:T(4,128)} %reduce.8) | data formatting | bytes 1572864
  327.2 8.4 %copy.131 = f32[12,8,8,16,16]{4,2,3,1,0:T(8,128)} copy(f32[12,8,8,16,16]{4,3,2,1,0:T(8,128)} %reshape.520) | data formatting | bytes 1572864 | tf_op jit(solution)/shard_map/reshape | solution.py:177
  341.0 37.1 %copy.122 = f32[1,3,4,16384]{2,0,1,3:T(1,128)} copy(f32[1,3,4,16384]{3,2,1,0:T(4,128)S(1)} %reshape.521) | data formatting | bytes 1572864 | tf_op jit(solution)/shard_map/reshape | solution.py:180
  378.1 86.9 %reduce.12 = f32[16384,3,4]{2,1,0:T(4,128)} reduce(f32[16384,3,1,4]{3,2,1,0:T(1,128)} %bitcast.211, f32[]{:T(128)} %broadcast.766), dimensions={2}, to_apply=%bitcast.174.reduce_sub_computation | reduce | bytes 1572868
  465.0 21.0 %reshape.538 = f32[8,1,24576]{2,1,0:T(1,128)} reshape(f32[16384,3,4]{2,1,0:T(4,128)} %reduce.12) | data formatting | bytes 1572864
  493.9 56.3 %reshape.535 = f32[16384,3,1,4]{3,2,1,0:T(1,128)} reshape(f32[8,24576]{1,0:T(8,128)S(1)} %reduce.9) | data formatting | bytes 1572864
  550.2 44.7 %copy.109 = f32[1,3,4,16384]{3,2,1,0:T(4,128)S(1)} copy(f32[1,3,4,16384]{2,0,1,3:T(1,128)} %bitcast.212) | data formatting | bytes 1572864 | tf_op jit(solution)/shard_map/all_to_all | solution.py:182
  597.2 6.9 copy.111
  604.2 11.6 %reduce.10 = f32[2048,3,32]{2,1,0:T(4,128)} reduce(f32[2048,3,1,32]{3,2,1,0:T(1,128)S(1)} %bitcast.218, f32[]{:T(128)} %broadcast.766), dimensions={2}, to_apply=%bitcast.172.reduce_sub_computation | reduce | bytes 1572868
  621.0 6.6 all-to-all-start.3
  631.3 56.1 %reshape.539 = f32[16384,3,1,4]{3,2,1,0:T(1,128)} reshape(f32[8,24576]{1,0:T(8,128)S(1)} %reduce.13) | data formatting | bytes 1572864
  687.4 44.7 %copy.123 = f32[1,3,4,16384]{3,2,1,0:T(4,128)S(1)} copy(f32[1,3,4,16384]{2,0,1,3:T(1,128)} %bitcast.213) | data formatting | bytes 1572864 | tf_op jit(solution)/shard_map/all_to_all | solution.py:182
  734.4 6.9 copy.125
  741.3 12.0 %reduce.14 = f32[2048,3,32]{2,1,0:T(4,128)} reduce(f32[2048,3,1,32]{3,2,1,0:T(1,128)S(1)} %bitcast.219, f32[]{:T(128)} %broadcast.766), dimensions={2}, to_apply=%bitcast.176.reduce_sub_computation | reduce | bytes 1572868
  758.6 7.2 all-to-all-start.7
  (171 shorter events, 226.0 us)
Async XLA Ops:
  1.7 20.4 %collective-permute-start = (f32[3,2,16,512]{3,2,1,0:T(8,128)S(1)}, f32[3,2,16,512]{3,2,1,0:T(8,128)S(1)}, u32[]{:S(2)}, u32[]{:S(2)}) collective-permute-start(f32[3,2,16,512]{3,2,1,0:T(8,128)S(1)} %get-tuple-element.89), channel_id=1, source_target_pairs={{16,0},{32,16},{48,32},{64,48},{80,64},{96,80},{112,96},{0,112},{1... | collective-permute-start | bytes 589832 | tf_op jit(solution)/shard_map/ppermute | solution.py:21
  6.7 15.0 %collective-permute-start.1 = (f32[3,2,16,512]{3,2,1,0:T(8,128)S(1)}, f32[3,2,16,512]{3,2,1,0:T(8,128)S(1)}, u32[]{:S(2)}, u32[]{:S(2)}) collective-permute-start(f32[3,2,16,512]{3,2,1,0:T(8,128)S(1)} %get-tuple-element.90), channel_id=1, source_target_pairs={{0,16},{16,32},{32,48},{48,64},{64,80},{80,96},{96,112},{112,0},{1... | collective-permute-start | bytes 589832 | tf_op jit(solution)/shard_map/ppermute | solution.py:18
  6.7 14.7 %copy-start.17 = (f32[3,8,16,512]{3,2,1,0:T(8,128)S(1)}, f32[3,8,16,512]{3,2,1,0:T(8,128)}, u32[]{:S(2)}) copy-start(f32[3,8,16,512]{3,2,1,0:T(8,128)} %param.17) | copy-start | bytes 2359300
  10.7 11.1 %copy-start = (f32[3,8,16,512]{3,2,1,0:T(8,128)S(1)}, f32[3,8,16,512]{3,2,1,0:T(8,128)}, u32[]{:S(2)}) copy-start(f32[3,8,16,512]{3,2,1,0:T(8,128)} %param.16) | copy-start | bytes 2359300
  12.4 27.9 %all-to-all-start.4 = ((f32[1,3,512,128]{3,0,1,2:T(1,128)}), f32[1,3,512,128]{3,0,1,2:T(1,128)S(1)}, u32[]{:S(2)}, u32[]{:S(2)}) async-start(f32[1,3,512,128]{3,0,1,2:T(1,128)} %copy.114), calls=%async_computation.4 | async-start | bytes 1572864 | tf_op jit(solution)/shard_map/all_to_all | solution.py:116
  21.6 15.0 %copy-start.1 = (f32[8,16,512]{2,1,0:T(8,128)}, f32[8,16,512]{2,1,0:T(8,128)S(1)}, u32[]{:S(2)}) copy-start(f32[8,16,512]{2,1,0:T(8,128)S(1)} %get-tuple-element.82) | copy-start | bytes 786436
  21.7 15.0 %copy-start.3 = (f32[8,16,512]{2,1,0:T(8,128)}, f32[8,16,512]{2,1,0:T(8,128)S(1)}, u32[]{:S(2)}) copy-start(f32[8,16,512]{2,1,0:T(8,128)S(1)} %get-tuple-element.85) | copy-start | bytes 786436
  21.7 15.0 %copy-start.7 = (f32[8,16,512]{2,1,0:T(8,128)}, f32[8,16,512]{2,1,0:T(8,128)S(1)}, u32[]{:S(2)}) copy-start(f32[8,16,512]{2,1,0:T(8,128)S(1)} %get-tuple-element.80) | copy-start | bytes 786436
  21.7 15.0 %copy-start.9 = (f32[8,16,512]{2,1,0:T(8,128)}, f32[8,16,512]{2,1,0:T(8,128)S(1)}, u32[]{:S(2)}) copy-start(f32[8,16,512]{2,1,0:T(8,128)S(1)} %get-tuple-element.81) | copy-start | bytes 786436
  21.7 15.0 %copy-start.11 = (f32[8,16,512]{2,1,0:T(8,128)}, f32[8,16,512]{2,1,0:T(8,128)S(1)}, u32[]{:S(2)}) copy-start(f32[8,16,512]{2,1,0:T(8,128)S(1)} %get-tuple-element.83) | copy-start | bytes 786436
  21.7 15.0 %copy-start.13 = (f32[8,16,512]{2,1,0:T(8,128)}, f32[8,16,512]{2,1,0:T(8,128)S(1)}, u32[]{:S(2)}) copy-start(f32[8,16,512]{2,1,0:T(8,128)S(1)} %get-tuple-element.84) | copy-start | bytes 786436
  22.3 9.6 %collective-permute-start.2 = (f32[3,12,2,512]{3,2,1,0:T(2,128)S(1)}, f32[3,12,2,512]{3,2,1,0:T(2,128)S(1)}, u32[]{:S(2)}, u32[]{:S(2)}) collective-permute-start(f32[3,12,2,512]{3,2,1,0:T(2,128)S(1)} %get-tuple-element.71), channel_id=1, source_target_pairs={{1,0},{2,1},{3,2},{4,3},{5,4},{6,5},{7,6},{8,7},{9,8},{10,9},{11,1... | collective-permute-start | bytes 442376 | tf_op jit(solution)/shard_map/ppermute | solution.py:21
  22.5 11.9 %collective-permute-start.3 = (f32[3,12,2,512]{3,2,1,0:T(2,128)S(1)}, f32[3,12,2,512]{3,2,1,0:T(2,128)S(1)}, u32[]{:S(2)}, u32[]{:S(2)}) collective-permute-start(f32[3,12,2,512]{3,2,1,0:T(2,128)S(1)} %get-tuple-element.72), channel_id=1, source_target_pairs={{0,1},{1,2},{2,3},{3,4},{4,5},{5,6},{6,7},{7,8},{8,9},{9,10},{10,1... | collective-permute-start | bytes 442376 | tf_op jit(solution)/shard_map/ppermute | solution.py:18
  40.4 21.3 %all-to-all-start = ((f32[1,3,512,128]{3,0,1,2:T(1,128)}), f32[1,3,512,128]{3,0,1,2:T(1,128)S(1)}, u32[]{:S(2)}, u32[]{:S(2)}) async-start(f32[1,3,512,128]{3,0,1,2:T(1,128)} %copy.100), calls=%async_computation | async-start | bytes 1572864 | tf_op jit(solution)/shard_map/all_to_all | solution.py:116
  61.7 17.5 %all-to-all-start.5 = ((f32[1,3,32,2048]{3,0,1,2:T(1,128)}), f32[1,3,32,2048]{3,0,1,2:T(1,128)S(1)}, u32[]{:S(2)}, u32[]{:S(2)}) async-start(f32[1,3,32,2048]{3,0,1,2:T(1,128)} %copy.117), calls=%async_computation.5 | async-start | bytes 1572864 | tf_op jit(solution)/shard_map/all_to_all | solution.py:115
  79.2 29.2 %all-to-all-start.1 = ((f32[1,3,32,2048]{3,0,1,2:T(1,128)}), f32[1,3,32,2048]{3,0,1,2:T(1,128)S(1)}, u32[]{:S(2)}, u32[]{:S(2)}) async-start(f32[1,3,32,2048]{3,0,1,2:T(1,128)} %copy.103), calls=%async_computation.1 | async-start | bytes 1572864 | tf_op jit(solution)/shard_map/all_to_all | solution.py:115
  313.9 172.1 %all-to-all-start.2 = ((f32[8,1,24576]{2,1,0:T(1,128)}), f32[8,1,24576]{2,1,0:T(1,128)S(1)}, u32[]{:S(2)}, u32[]{:S(2)}) async-start(f32[8,1,24576]{2,1,0:T(1,128)} %reshape.534), calls=%async_computation.2 | async-start | bytes 1572864 | tf_op jit(solution)/shard_map/all_to_all | solution.py:182
  486.0 135.0 %all-to-all-start.6 = ((f32[8,1,24576]{2,1,0:T(1,128)}), f32[8,1,24576]{2,1,0:T(1,128)}, u32[]{:S(2)}, u32[]{:S(2)}) async-start(f32[8,1,24576]{2,1,0:T(1,128)} %reshape.538), calls=%async_computation.6 | async-start | bytes 1572864 | tf_op jit(solution)/shard_map/all_to_all | solution.py:182
  621.0 137.6 %all-to-all-start.3 = ((f32[16,1,12288]{2,1,0:T(1,128)}), f32[16,1,12288]{2,1,0:T(1,128)}, u32[]{:S(2)}, u32[]{:S(2)}) async-start(f32[16,1,12288]{2,1,0:T(1,128)} %reshape.536), calls=%async_computation.3 | async-start | bytes 1572864 | tf_op jit(solution)/shard_map/all_to_all | solution.py:181
  758.6 34.9 %all-to-all-start.7 = ((f32[16,1,12288]{2,1,0:T(1,128)}), f32[16,1,12288]{2,1,0:T(1,128)}, u32[]{:S(2)}, u32[]{:S(2)}) async-start(f32[16,1,12288]{2,1,0:T(1,128)} %reshape.540), calls=%async_computation.7 | async-start | bytes 1572864 | tf_op jit(solution)/shard_map/all_to_all | solution.py:181
  823.5 7.8 collective-permute-start.6
  827.4 5.6 collective-permute-start.7
  827.5 10.4 %collective-permute-start.5 = (f32[3,2,16,512]{3,2,1,0:T(8,128)S(1)}, f32[3,2,16,512]{3,2,1,0:T(8,128)S(1)}, u32[]{:S(2)}, u32[]{:S(2)}) collective-permute-start(f32[3,2,16,512]{3,2,1,0:T(8,128)S(1)} %get-tuple-element.69), channel_id=1, source_target_pairs={{16,0},{32,16},{48,32},{64,48},{80,64},{96,80},{112,96},{0,112},{1... | collective-permute-start | bytes 589832 | tf_op jit(solution)/shard_map/ppermute | solution.py:21
  831.3 6.6 collective-permute-start.4
  (14 other events, 53.9 us)
where the time goes:
time: 854 us; the launch traced here: 841 us
  local copies, waits for them, and re-layouts  460 us (54%)
  other arithmetic  224 us (26%)
  starting transfers between devices  63.7 us (7%)
  matrix products  53 us (6%)
  waiting for transfers between devices  38.2 us (4%)
    unnamed x4, other arithmetic  197 us
    unnamed x57, local copies, waits for them, and re-layouts  184 us
    all_to_all x8, local copies, waits for them, and re-layouts, project(): lax.all_to_all(flattened_back, 'gx', split_axis=3, concat_axis=2, tiled=T...  108 us
    reshape x4, local copies, waits for them, and re-layouts, project(): flattened_back = regrouped.reshape(groups, 3, mode_count, grid_x * grid_y)  85 us
    dot_general x16, matrix products, along_y(): return jnp.einsum('bky,yl->bkl', planes, table, precision=highest)  28.6 us
    reshape x4, local copies, waits for them, and re-layouts, project(): physical.reshape(groups * 3 * mode_count, parts_x, cells_x, parts_y, cell...  25 us
  transfers between devices with their start and end apart: 16, of which 6 were waited for; matrix products, arithmetic and copies ran while one was open for 59% of the time, Pallas kernels for 0%

commit v1 on v0

v1 whole, which is shorter than its diff:
```python
import functools
import math

import jax
import jax.numpy as jnp
import ml_dtypes
import numpy as np
from jax import lax
from jax.experimental import pallas as pl
from jax.experimental.pallas import tpu as pltpu
from jax.sharding import PartitionSpec as P

MESH = pl.DeviceIdType.MESH
BX, BY = 8, 16
GX, GY = 8, 16
NX, NY, NZ = 64, 256, 512
DEVICES = GX * GY
OWNED = NZ // DEVICES
SLOTS = 64
f32, bf16 = jnp.float32, jnp.bfloat16


def fourier(n):
    place = np.arange(n)
    basis = np.zeros((n, n))
    freq = np.zeros(n)
    for column in range(n):
        k = (column + 1) // 2
        angle = 2.0 * math.pi * k * place / n
        if column == 0 or k == n // 2:
            basis[:, column] = np.cos(angle) / math.sqrt(n)
        else:
            basis[:, column] = (np.cos(angle) if column % 2 else np.sin(angle)) * math.sqrt(2.0 / n)
        freq[column] = 2.0 - 2.0 * math.cos(2.0 * math.pi * k / n)
    return basis, freq


def split_const(matrix):
    high = matrix.astype(ml_dtypes.bfloat16)
    low = (matrix - high.astype(np.float64)).astype(ml_dtypes.bfloat16)
    return high, low


def tables():
    j, k = np.arange(BX), np.arange(BY)
    sin_x = math.sqrt(2.0 / BX) * np.sin(math.pi * np.outer(j, j) / BX)
    sin_y = math.sqrt(2.0 / BY) * np.sin(math.pi * np.outer(k, k) / BY)
    sin_x[0], sin_x[:, 0], sin_y[0], sin_y[:, 0] = 0.0, 0.0, 0.0, 0.0
    sine = np.kron(sin_x, sin_y)
    mu = (2.0 - 2.0 * np.cos(math.pi * j / BX))[:, None] + (2.0 - 2.0 * np.cos(math.pi * k / BY))
    mu = np.repeat(mu.reshape(-1, 1), 128, axis=1)
    near = np.zeros((SLOTS, BX * BY))
    own = np.zeros((SLOTS, BX * BY))
    for y in range(BY):
        own[y, y] = 1.0
        if y:
            near[y] = sine[1 * BY + y]
            near[16 + y] = sine[(BX - 1) * BY + y]
    for x in range(1, BX):
        own[32 + x, x * BY] = 1.0
        near[32 + x] = sine[x * BY + 1]
        near[40 + x] = sine[x * BY + BY - 1]
    to_slots = np.concatenate([near, own], 1)
    from_slots = np.concatenate([sine, own.T], 1)
    qx, lx = fourier(NX)
    qy, ly = fourier(NY)
    w1 = np.zeros((GY, SLOTS, 3, 256))
    for g in range(GY):
        w1[g, 0:16, 0] = qy[16 * g : 16 * g + 16]
        w1[g, 16:32, 1] = qy[16 * g : 16 * g + 16]
        for x in range(BX):
            for kind in range(2):
                w1[g, 32 + 8 * kind + x, 2, x * 32 + kind * 16 + g] = 1.0
    w1 = w1.reshape(GY * SLOTS, 768)
    rows = np.zeros((2, NX, OWNED, 2, 2, GX, OWNED))
    cols = np.zeros((2, NX, OWNED, BX, 2, GX, OWNED))
    for group in range(2):
        for mode in range(OWNED):
            for g in range(GX):
                for kind in range(2):
                    rows[group, :, mode, kind, group, g, mode] = qx[8 * (g + kind) % NX]
                for x in range(BX):
                    cols[group, :, mode, x, group, g, mode] = qx[8 * g + x]
    rows = rows.reshape(512, 128)
    cols = cols.reshape(512, 512)
    wc = np.stack([qy[0::16], np.roll(qy[0::16], -1, axis=0)]).reshape(32, 256)
    lam_x = np.repeat(np.broadcast_to(lx[None, :, None], (2, NX, OWNED)).reshape(512, 1), 128, axis=1)
    lam_y = ly[None, :]
    split = [sine, to_slots, near.T, from_slots, w1, rows, rows.T, cols, cols.T, wc, wc.T]
    out = []
    for matrix in split:
        out.extend(split_const(np.ascontiguousarray(matrix)))
    plain = [mu.astype(np.float32), lam_x.astype(np.float32), lam_y.astype(np.float32)]
    return [jnp.asarray(t) for t in out + plain]


def halves(value):
    high = value.astype(bf16)
    low = (value - high.astype(f32)).astype(bf16)
    return high, low


def dot(a, b, nt=False):
    dims = (((1,), (1 if nt else 0,)), ((), ()))
    return lax.dot_general(a, b, dims, preferred_element_type=f32)


def dot3(a, b, nt=False):
    return dot(a[0], b[0], nt) + (dot(a[0], b[1], nt) + dot(a[1], b[0], nt))


def wide(column, lanes):
    return jnp.concatenate([column] * (lanes // 128), axis=1)


TAPS = ((-2, 1.0, 1.0), (-1, -8.0, -4.0), (0, 0.0, 6.0), (1, 8.0, -4.0), (2, -1.0, 1.0))


def weights(speed):
    size = jnp.abs(speed)
    out = {}
    for offset, central, hyper in TAPS:
        out[offset] = hyper * size + central * speed if central else hyper * size
    return out


def moved(value, offset, axis):
    n = value.shape[axis]
    if axis == 1:
        rolled = pltpu.roll(value, (-offset) % n, 1)
    else:
        rolled = jnp.roll(value, -offset, 0)
    place = lax.broadcasted_iota(jnp.int32, value.shape, axis)
    keep = place < n - offset if offset > 0 else place >= -offset
    return jnp.where(keep, rolled, 0.0)


def kernel(
    vel, adv, cot, height, section, vm_ref, vt_ref, rate_row, rate_s,
    sine_h, sine_l, ts_h, ts_l, nt_h, nt_l, fs_h, fs_l, w1_h, w1_l, rw_h, rw_l, rt_h, rt_l,
    cl_h, cl_l, ct_h, ct_l, wc_h, wc_l, wt_h, wt_l, mu_ref, lamx_ref, lamy_ref,
    next_ref, adj_ref,
    vb, sv, lhs, vh, vl, th, tl, ys, yr, sb, rbuf, ob, rb, xs, cx, gp, sxp, cxs, cxr, cys, cyr,
    d_ref, p1_ref, ie_ref,
    a_send, a_recv, h_send, h_recv, l_sem,
):
    gx, gy = lax.axis_index("gx"), lax.axis_index("gy")
    me = gx * GY + gy
    left_x, right_x = lax.rem(gx + GX - 1, GX), lax.rem(gx + 1, GX)
    left_y, right_y = lax.rem(gy + GY - 1, GY), lax.rem(gy + 1, GY)

    def other(i):
        t = lax.rem(me + i, DEVICES)
        return t, lax.div(t, GY), lax.rem(t, GY)

    barrier = pltpu.get_barrier_semaphore()

    def greet(i, carry):
        _, tx, ty = other(i)
        pl.semaphore_signal(barrier, inc=1, device_id=(tx, ty), device_id_type=MESH)
        return carry

    lax.fori_loop(1, DEVICES, greet, 0)

    for c in range(3):
        for x in range(BX):
            ys[0, c, 2 * x : 2 * x + 2, :] = vel[c, x, 0:2, :]
            ys[1, c, 2 * x : 2 * x + 2, :] = vel[c, x, BY - 2 : BY, :]

    pl.semaphore_wait(barrier, DEVICES - 1)

    def remote(src, dst, n, x, y):
        return pltpu.make_async_remote_copy(
            src_ref=src, dst_ref=dst, send_sem=h_send.at[n], recv_sem=h_recv.at[n],
            device_id=(x, y), device_id_type=MESH,
        )

    halo = [
        remote(vel.at[:, pl.ds(0, 2)], vb.at[:, pl.ds(BX + 2, 2), pl.ds(8, BY)], 0, left_x, gy),
        remote(vel.at[:, pl.ds(BX - 2, 2)], vb.at[:, pl.ds(0, 2), pl.ds(8, BY)], 1, right_x, gy),
        remote(ys.at[0], yr.at[1], 2, gx, left_y),
        remote(ys.at[1], yr.at[0], 3, gx, right_y),
    ]
    for copy in halo:
        copy.start()

    for c in range(3):
        vb[c, 2 : BX + 2, 8 : 8 + BY, :] = vel[c]
    for full, high, low in ((vm_ref, vh, vl), (vt_ref, th, tl)):
        for i in range(0, NZ, 64):
            h, l = halves(full[i : i + 64, :])
            high[i : i + 64, :] = h
            low[i : i + 64, :] = l
    ie_ref[...] = 1.0 / (wide(mu_ref[...], NZ) + rate_row[...])

    number = section[0]
    part = lax.rem(number, 3)
    step = lax.div(number, 3).astype(f32)
    fraction = jnp.where(part == 0, f32(1.0 / 3.0), jnp.where(part == 1, f32(0.5), f32(1.0)))
    factor = (f32(0.2) + step * f32(0.2 / 63.0)) * fraction
    scale = factor * f32(-1.0 / 12.0)

    levels = lax.broadcasted_iota(jnp.int32, (BY, NZ), 1).astype(f32)
    diagonal = lax.broadcasted_iota(jnp.int32, (BY, BY), 0) == lax.broadcasted_iota(
        jnp.int32, (BY, BY), 1
    )

    def fluid_at(x):
        row = height[pl.ds(x, 1), :].astype(f32)
        column = jnp.sum(jnp.where(diagonal, row, 0.0), axis=1, keepdims=True)
        return (levels >= column).astype(f32)

    def left_sides(group, field):
        for x in range(BX):
            f0 = field[0, x]
            if x:
                f0 = f0 - field[0, x - 1]
            f1 = field[1, x]
            lhs[group, BY * x : BY * x + BY, :] = f0 + (f1 - moved(f1, -1, 0))
            lhs[group, 144 + x : 145 + x, :] = -field[1, x, BY - 1 : BY, :]
        lhs[group, 128:144, :] = -field[0, BX - 1]
        lhs[group, 152:160, :] = jnp.zeros((8, NZ), f32)

    def forward(group, field):
        left_sides(group, field)
        wide_rows = dot3(halves(lhs[group]), (vh[...], vl[...]))
        tilted = dot3(halves(field[2].reshape(BX * BY, NZ)), (th[...], tl[...]))
        d = wide_rows[:128] + tilted
        d_parts = halves(d)
        p1 = dot3((sine_h[...], sine_l[...]), d_parts)
        p1_ref[group] = p1
        w = halves(p1 * ie_ref[...])
        both = (
            jnp.concatenate([w[0], d_parts[0]], axis=0),
            jnp.concatenate([w[1], d_parts[1]], axis=0),
        )
        s = dot3((ts_h[...], ts_l[...]), both)
        d_ref[group * SLOTS : group * SLOTS + 64, :] = s
        d_ref[group * SLOTS + 16 : group * SLOTS + 32, :] += wide_rows[128:144]
        d_ref[group * SLOTS + 40 : group * SLOTS + 48, :] += wide_rows[144:152]

    forward(1, cot)

    for copy in halo:
        copy.wait()
    for c in range(3):
        for x in range(BX):
            vb[c, x + 2, 6:8, :] = yr[0, c, 2 * x : 2 * x + 2, :]
            vb[c, x + 2, 8 + BY : 10 + BY, :] = yr[1, c, 2 * x : 2 * x + 2, :]

    def section_row(x, carry):
        fluid = fluid_at(x)
        kx, ky, kz = weights(adv[0, x]), weights(adv[1, x]), weights(adv[2, x])
        for c in range(3):
            center = vb[c, x + 2, 8 : 8 + BY, :]
            total = center * (kx[0] + ky[0] + kz[0])
            for offset in (-2, -1, 1, 2):
                total = total + kx[offset] * vb[c, x + 2 + offset, 8 : 8 + BY, :]
                total = total + ky[offset] * vb[c, x + 2, 8 + offset : 8 + BY + offset, :]
                total = total + kz[offset] * moved(center, offset, 1)
            sv[c, x] = fluid * (center + scale * total)
        return carry

    lax.fori_loop(0, BX, section_row, 0)
    forward(0, sv)

    for i in range(4):
        sb[128 * i : 128 * i + 128, :] = d_ref[:, 128 * i : 128 * i + 128].T

    def exchange(n, src, dst, src_row, dst_row):
        def start(i, carry):
            t, tx, ty = other(i)
            pltpu.make_async_remote_copy(
                src_ref=src.at[pl.ds(src_row(t, tx, ty) * OWNED, OWNED)],
                dst_ref=dst.at[pl.ds(dst_row * OWNED, OWNED)],
                send_sem=a_send.at[n], recv_sem=a_recv.at[n],
                device_id=(tx, ty), device_id_type=MESH,
            ).start()
            return carry

        lax.fori_loop(1, DEVICES, start, 0)
        local = pltpu.make_async_copy(
            src.at[pl.ds(src_row(me, gx, gy) * OWNED, OWNED)],
            dst.at[pl.ds(dst_row * OWNED, OWNED)],
            l_sem.at[n],
        )
        local.start()
        local.wait()
        whole = pltpu.make_async_remote_copy(
            src_ref=src.at[pl.ds(0, (DEVICES - 1) * OWNED)],
            dst_ref=dst.at[pl.ds(0, (DEVICES - 1) * OWNED)],
            send_sem=a_send.at[n], recv_sem=a_recv.at[n],
            device_id=(right_x, gy), device_id_type=MESH,
        )
        whole.wait_send()
        whole.wait_recv()

    place = gy * GX + gx
    exchange(0, sb, rbuf, lambda t, tx, ty: t, place)

    low_lanes = lax.broadcasted_iota(jnp.int32, (32, 128), 1) < SLOTS
    for pair in range(GY // 2):
        a = rbuf[64 * pair : 64 * pair + 32, :]
        b = rbuf[64 * pair + 32 : 64 * pair + 64, :]
        xs[0:32, 128 * pair : 128 * pair + 128] = jnp.where(low_lanes, a, pltpu.roll(b, 64, 1))
        xs[32:64, 128 * pair : 128 * pair + 128] = jnp.where(low_lanes, pltpu.roll(a, 64, 1), b)
    y1 = dot3(halves(xs[...]), (w1_h[...], w1_l[...]))
    stacked = jnp.concatenate([y1[:, 0:256], y1[:, 256:512]], axis=0)
    for x in range(BX):
        cx[64 * x : 64 * x + 64, :] = y1[:, 512 + 32 * x : 544 + 32 * x]
    hat = dot3((rw_h[...], rw_l[...]), halves(stacked))
    inner = dot3((cl_h[...], cl_l[...]), halves(cx[...]))
    hat = hat + dot3(halves(inner), (wc_h[...], wc_l[...]))
    row_mode = lax.rem(lax.broadcasted_iota(jnp.int32, (512, 128), 0), OWNED)
    rate = jnp.zeros((512, 128), f32)
    for m in range(OWNED):
        rate = jnp.where(row_mode == m, rate_s[me * OWNED + m], rate)
    hat = hat / (wide(rate + lamx_ref[...], 256) + lamy_ref[...])
    hat_parts = halves(hat)
    back = dot3((rt_h[...], rt_l[...]), hat_parts)
    inner = dot3(hat_parts, (wt_h[...], wt_l[...]))
    cx[...] = dot3((ct_h[...], ct_l[...]), halves(inner))
    parts = [back[0:64], back[64:128]] + [cx[64 * x : 64 * x + 64, :] for x in range(BX)]
    xs[...] = dot3(halves(jnp.concatenate(parts, axis=1)), (w1_h[...], w1_l[...]), nt=True)
    for pair in range(GY // 2):
        p = xs[0:32, 128 * pair : 128 * pair + 128]
        q = xs[32:64, 128 * pair : 128 * pair + 128]
        ob[64 * pair : 64 * pair + 32, :] = jnp.where(low_lanes, p, pltpu.roll(q, 64, 1))
        ob[64 * pair + 32 : 64 * pair + 64, :] = jnp.where(low_lanes, pltpu.roll(p, 64, 1), q)

    exchange(1, ob, rb, lambda t, tx, ty: ty * GX + tx, me)

    for i in range(4):
        d_ref[:, 128 * i : 128 * i + 128] = rb[128 * i : 128 * i + 128, :].T

    def backward(group):
        u = d_ref[group * SLOTS : group * SLOTS + SLOTS, :]
        u_parts = halves(u)
        inside = (p1_ref[group] + dot3((nt_h[...], nt_l[...]), u_parts)) * ie_ref[...]
        in_parts = halves(inside)
        both = (
            jnp.concatenate([in_parts[0], u_parts[0]], axis=0),
            jnp.concatenate([in_parts[1], u_parts[1]], axis=0),
        )
        phi = dot3((fs_h[...], fs_l[...]), both)
        ext = jnp.concatenate([phi, u[16:32], u[40:48], jnp.zeros((8, NZ), f32)], axis=0)
        lhs[group] = dot3(halves(ext), (vh[...], vl[...]), nt=True)
        return dot3(halves(phi), (th[...], tl[...]), nt=True)

    def corrections(group, x):
        here = lhs[group, BY * x : BY * x + BY, :]
        after = lhs[group, BY * x + BY : BY * x + 2 * BY, :]
        last = lax.broadcasted_iota(jnp.int32, (BY, NZ), 0) == BY - 1
        side = jnp.where(last, lhs[group, 144 + x : 145 + x, :], jnp.roll(here, -1, 0))
        return here - after, here - side

    tilted = backward(1)
    for x in range(BX):
        fluid = fluid_at(x)
        c0, c1 = corrections(1, x)
        gp[0, x + 2] = fluid * (cot[0, x] - c0)
        gp[1, x + 2] = fluid * (cot[1, x] - c1)
        gp[2, x + 2] = fluid * (cot[2, x] - tilted[BY * x : BY * x + BY])
        sxp[x + 2] = adv[0, x]
    nothing = jnp.zeros((2, BY, NZ), f32)
    for c in range(3):
        gp[c, 0:2] = nothing
        gp[c, BX + 2 : BX + 4] = nothing
    sxp[0:2] = nothing
    sxp[BX + 2 : BX + 4] = nothing

    k0, k1 = weights(adv[0, 0]), weights(adv[0, 1])
    k6, k7 = weights(adv[0, BX - 2]), weights(adv[0, BX - 1])
    for c in range(3):
        g0, g1, g6, g7 = gp[c, 2], gp[c, 3], gp[c, BX], gp[c, BX + 1]
        cxs[0, c, 0] = k0[-2] * g0
        cxs[0, c, 1] = k0[-1] * g0 + k1[-2] * g1
        cxs[1, c, 0] = k7[1] * g7 + k6[2] * g6
        cxs[1, c, 1] = k7[2] * g7
    for x in range(BX):
        k = weights(adv[1, x])
        for c in range(3):
            g = gp[c, x + 2]
            one, two = k[-1] * g, k[-2] * g
            cys[0, c, 2 * x : 2 * x + 1, :] = two[0:1]
            cys[0, c, 2 * x + 1 : 2 * x + 2, :] = one[0:1] + two[1:2]
            one, two = k[1] * g, k[2] * g
            cys[1, c, 2 * x : 2 * x + 1, :] = one[BY - 1 : BY] + two[BY - 2 : BY - 1]
            cys[1, c, 2 * x + 1 : 2 * x + 2, :] = two[BY - 1 : BY]
    edges = [
        remote(cxs.at[0], cxr.at[1], 4, left_x, gy),
        remote(cxs.at[1], cxr.at[0], 5, right_x, gy),
        remote(cys.at[0], cyr.at[1], 6, gx, left_y),
        remote(cys.at[1], cyr.at[0], 7, gx, right_y),
    ]
    for copy in edges:
        copy.start()

    tilted = backward(0)
    for x in range(BX):
        c0, c1 = corrections(0, x)
        next_ref[0, x] = sv[0, x] - c0
        next_ref[1, x] = sv[1, x] - c1
        next_ref[2, x] = sv[2, x] - tilted[BY * x : BY * x + BY]

    def adjoint_row(x, carry):
        kx = {}
        for offset in (-2, -1, 0, 1, 2):
            kx[offset] = weights(sxp[x + 2 - offset])[offset]
        ky, kz = weights(adv[1, x]), weights(adv[2, x])
        for c in range(3):
            center = gp[c, x + 2]
            total = center * (kx[0] + ky[0] + kz[0])
            for offset in (-2, -1, 1, 2):
                total = total + kx[offset] * gp[c, x + 2 - offset]
                total = total + moved(ky[offset] * center, -offset, 0)
                total = total + moved(kz[offset] * center, -offset, 1)
            adj_ref[c, x] = center + scale * total
        return carry

    lax.fori_loop(0, BX, adjoint_row, 0)
    for copy in edges:
        copy.wait()
    for c in range(3):
        for n in range(2):
            adj_ref[c, n] += scale * cxr[0, c, n]
            adj_ref[c, BX - 2 + n] += scale * cxr[1, c, n]
        for x in range(BX):
            adj_ref[c, x, 0:2, :] += scale * cyr[0, c, 2 * x : 2 * x + 2, :]
            adj_ref[c, x, BY - 2 : BY, :] += scale * cyr[1, c, 2 * x : 2 * x + 2, :]


def per_device(
    velocity_now, advecting, cotangent, building_height, section_index,
    vertical_modes, vertical_tilt, mode_rates,
):
    constants = tables()
    vmem = pl.BlockSpec(memory_space=pltpu.VMEM)
    smem = pl.BlockSpec(memory_space=pltpu.SMEM)
    field = jax.ShapeDtypeStruct((3, BX, BY, NZ), f32)
    return pl.pallas_call(
        kernel,
        out_shape=(field, field),
        in_specs=[vmem, vmem, vmem, vmem, smem, vmem, vmem, vmem, smem] + [vmem] * len(constants),
        out_specs=(vmem, vmem),
        scratch_shapes=[
            pltpu.VMEM((3, BX + 4, 32, NZ), f32),
            pltpu.VMEM((3, BX, BY, NZ), f32),
            pltpu.VMEM((2, 160, NZ), f32),
            pltpu.VMEM((NZ, NZ), bf16),
            pltpu.VMEM((NZ, NZ), bf16),
            pltpu.VMEM((NZ, NZ), bf16),
            pltpu.VMEM((NZ, NZ), bf16),
            pltpu.VMEM((2, 3, 16, NZ), f32),
            pltpu.VMEM((2, 3, 16, NZ), f32),
            pltpu.VMEM((NZ, 128), f32),
            pltpu.VMEM((NZ, 128), f32),
            pltpu.VMEM((NZ, 128), f32),
            pltpu.VMEM((NZ, 128), f32),
            pltpu.VMEM((64, 1024), f32),
            pltpu.VMEM((512, 32), f32),
            pltpu.VMEM((3, BX + 4, BY, NZ), f32),
            pltpu.VMEM((BX + 4, BY, NZ), f32),
            pltpu.VMEM((2, 3, 2, BY, NZ), f32),
            pltpu.VMEM((2, 3, 2, BY, NZ), f32),
            pltpu.VMEM((2, 3, 16, NZ), f32),
            pltpu.VMEM((2, 3, 16, NZ), f32),
            pltpu.VMEM((128, NZ), f32),
            pltpu.VMEM((2, 128, NZ), f32),
            pltpu.VMEM((128, NZ), f32),
            pltpu.SemaphoreType.DMA((2,)),
            pltpu.SemaphoreType.DMA((2,)),
            pltpu.SemaphoreType.DMA((8,)),
            pltpu.SemaphoreType.DMA((8,)),
            pltpu.SemaphoreType.DMA((2,)),
        ],
        compiler_params=pltpu.CompilerParams(
            collective_id=0, has_side_effects=True, vmem_limit_bytes=56 * 1024 * 1024
        ),
    )(
        velocity_now, advecting, cotangent, building_height, section_index,
        vertical_modes, vertical_tilt, mode_rates.reshape(1, NZ), mode_rates, *constants,
    )


def solution(mesh):
    blocks = P(None, "gx", "gy", None)
    return jax.shard_map(
        per_device,
        mesh=mesh,
        in_specs=(blocks, blocks, blocks, P("gx", "gy"), P(), P(), P(), P()),
        out_specs=(blocks, blocks),
        check_vma=False,
    )
```

time: 854 us -> 65.6 us (0.08); the launches traced: 841 us -> 65.5 us
  local copies, waits for them, and re-layouts: 460 us -> 3.04 us
  other arithmetic: 224 us -> 0 us
  starting transfers between devices: 63.7 us -> 0 us
  Pallas kernels: 0 us -> 61.2 us
  matrix products: 53 us -> 0 us
  waiting for transfers between devices: 38.2 us -> 0 us
    unnamed x4 -> x0, other arithmetic: 197 us -> none
    unnamed x57 -> x4, local copies, waits for them, and re-layouts: 184 us -> 3.04 us
    reshape x12 -> x0, local copies, waits for them, and re-layouts: 128 us -> none  [the longest x4 85 us: project(): flattened_back = regrouped.reshape(groups, 3, mode_count, grid_x * grid_y)]
    all_to_all x22 -> x0, local copies, waits for them, and re-layouts: 128 us -> none  [the longest x8 108 us: project(): lax.all_to_all(flattened_back, 'gx', split_axis=3, concat_axis=2, tiled=T...]
    pallas_call x0 -> x1, Pallas kernels: none -> 61.2 us  [per_device(): pl.pallas_call(kernel, out_shape=(field, field), in_specs=[vmem, vmem, vm...]
    all_to_all x8 -> x0, starting transfers between devices: 48.3 us -> none  [the longest x2 15.4 us: project(): lax.all_to_all(flattened, 'gy', split_axis=2, concat_axis=3, tiled=True)]
    dot_general x26 -> x0, matrix products: 42 us -> none  [the longest x16 28.6 us: along_y(): return jnp.einsum('bky,yl->bkl', planes, table, precision=highest)]
    all_to_all x8 -> x0, waiting for transfers between devices: 23.1 us -> none  [the longest x2 12.7 us: project(): lax.all_to_all(flattened, 'gy', split_axis=2, concat_axis=3, tiled=True)]
  transfers between devices with their start and end apart: 16 -> 0, of which waited for: 6 -> 0; matrix products, arithmetic and copies ran while one was open for 59% -> 0% of each run, Pallas kernels for 0% -> 0%
where the time goes in v1:
time: 65.6 us; the launch traced here: 65.5 us
  Pallas kernels  61.2 us (93%)
  local copies, waits for them, and re-layouts  3.04 us (5%)
  between operations  1.29 us (2%)
    pallas_call x1, Pallas kernels, per_device(): pl.pallas_call(kernel, out_shape=(field, field), in_specs=[vmem, vmem, vm...  61.2 us
    unnamed x4, local copies, waits for them, and re-layouts  3.04 us

profile of v1, /device:TPU:1, one launch (start us, length us, event | category | flops | bytes accessed | tf_op | source)
XLA Modules:
  0.0 65.5 jit_solution(10105154523542672956)
XLA Ops:
  1.3 61.2 %shard_map.320 = (f32[3,8,16,512]{3,2,1,0:T(8,128)}, f32[3,8,16,512]{3,2,1,0:T(8,128)}) custom-call(f32[3,8,16,512]{3,2,1,0:T(8,128)} %vel.1, f32[3,8,16,512]{3,2,1,0:T(8,128)} %adv.1, f32[3,8,16,512]{3,2,1,0:T(8,128)} %cot.1, s32[8,16]{1,0:T(8,128)} %height.1, s32[1]{0:T(128)S(6)} %copy.37.section, f32[512,512]{1,0:T(8,128)} %vm_ref.1, f32[512,512]{1,0:T(8,128)} %vt_ref.1, ...), custom_call_target="tpu_custom_call" | custom-call | tf_op jit(solution)/shard_map/pallas_call | solution.py:441
  62.5 0.0 copy-start
  62.5 2.2 %copy.38 = f32[3,8,16,512]{3,2,1,0:T(8,128)} copy(f32[3,8,16,512]{3,2,1,0:T(8,128)} %get-tuple-element.4) | data formatting | bytes 1572864
  64.6 0.0 copy-done
  64.6 0.9 %copy.39 = f32[3,8,16,512]{3,2,1,0:T(8,128)} copy(f32[3,8,16,512]{3,2,1,0:T(8,128)S(1)} %copy-done) | data formatting | bytes 1572864
Async XLA Ops:
  62.5 2.2 %copy-start = (f32[3,8,16,512]{3,2,1,0:T(8,128)S(1)}, f32[3,8,16,512]{3,2,1,0:T(8,128)}, u32[]{:S(2)}) copy-start(f32[3,8,16,512]{3,2,1,0:T(8,128)} %get-tuple-element.5) | copy-start | bytes 2359300

commit v2 on v1

--- a/solution.py
+++ b/solution.py
@@ -15,7 +15,8 @@
 GX, GY = 8, 16
 NX, NY, NZ = 64, 256, 512
 DEVICES = GX * GY
-OWNED = NZ // DEVICES
+OWNERS = DEVICES // 2
+OWNED = NZ // OWNERS // 2
 SLOTS = 64
 f32, bf16 = jnp.float32, jnp.bfloat16
 
@@ -64,14 +65,12 @@
     from_slots = np.concatenate([sine, own.T], 1)
     qx, lx = fourier(NX)
     qy, ly = fourier(NY)
-    w1 = np.zeros((GY, SLOTS, 3, 256))
+    order = np.zeros((GY, 2, BX, BX, 2, GY))
     for g in range(GY):
-        w1[g, 0:16, 0] = qy[16 * g : 16 * g + 16]
-        w1[g, 16:32, 1] = qy[16 * g : 16 * g + 16]
-        for x in range(BX):
-            for kind in range(2):
-                w1[g, 32 + 8 * kind + x, 2, x * 32 + kind * 16 + g] = 1.0
-    w1 = w1.reshape(GY * SLOTS, 768)
+        for kind in range(2):
+            for x in range(BX):
+                order[g, kind, x, x, kind, g] = 1.0
+    order = order.reshape(256, 256)
     rows = np.zeros((2, NX, OWNED, 2, 2, GX, OWNED))
     cols = np.zeros((2, NX, OWNED, BX, 2, GX, OWNED))
     for group in range(2):
@@ -86,12 +85,14 @@
     wc = np.stack([qy[0::16], np.roll(qy[0::16], -1, axis=0)]).reshape(32, 256)
     lam_x = np.repeat(np.broadcast_to(lx[None, :, None], (2, NX, OWNED)).reshape(512, 1), 128, axis=1)
     lam_y = ly[None, :]
-    split = [sine, to_slots, near.T, from_slots, w1, rows, rows.T, cols, cols.T, wc, wc.T]
     out = []
-    for matrix in split:
+    for matrix in [sine, to_slots, near.T, from_slots, qy, qy.T, rows, rows.T, wc, wc.T]:
         out.extend(split_const(np.ascontiguousarray(matrix)))
+    for matrix in [order, order.T]:
+        out.append(matrix.astype(ml_dtypes.bfloat16))
+    large = np.stack(split_const(cols) + split_const(cols.T))
     plain = [mu.astype(np.float32), lam_x.astype(np.float32), lam_y.astype(np.float32)]
-    return [jnp.asarray(t) for t in out + plain]
+    return [jnp.asarray(t) for t in [large] + out + plain]
 
 
 def halves(value):
@@ -103,6 +104,25 @@
 def dot(a, b, nt=False):
     dims = (((1,), (1 if nt else 0,)), ((), ()))
     return lax.dot_general(a, b, dims, preferred_element_type=f32)
+
+
+def dot_narrow(a, b):
+    n = b[0].shape[1]
+    both = dot(a[0], jnp.concatenate([b[0], b[1]], axis=1))
+    return both[:, :n] + (both[:, n:] + dot(a[1], b[0]))
+
+
+def regroup(blocks):
+    blocks = list(blocks)
+    group = lax.broadcasted_iota(jnp.int32, blocks[0].shape, 1) // 16
+    for step in (4, 2, 1):
+        low = (group & step) == 0
+        for i in range(8):
+            if not i & step:
+                a, b = blocks[i], blocks[i + step]
+                blocks[i] = jnp.where(low, a, pltpu.roll(b, 16 * step, 1))
+                blocks[i + step] = jnp.where(low, pltpu.roll(a, 128 - 16 * step, 1), b)
+    return blocks
 
 
 def dot3(a, b, nt=False):
@@ -136,38 +156,50 @@
 
 
 def kernel(
-    vel, adv, cot, height, section, vm_ref, vt_ref, rate_row, rate_s,
-    sine_h, sine_l, ts_h, ts_l, nt_h, nt_l, fs_h, fs_l, w1_h, w1_l, rw_h, rw_l, rt_h, rt_l,
-    cl_h, cl_l, ct_h, ct_l, wc_h, wc_l, wt_h, wt_l, mu_ref, lamx_ref, lamy_ref,
+    vel_h, adv_h, cot_h, height, section, vm_h, vt_h, rate_row, rate_s, large_h,
+    sine_h, sine_l, ts_h, ts_l, nt_h, nt_l, fs_h, fs_l, qy_h, qy_l, qt_h, qt_l, rw_h, rw_l, rt_h, rt_l,
+    wc_h, wc_l, wt_h, wt_l, order_ref, ordert_ref, mu_ref, lamx_ref, lamy_ref,
     next_ref, adj_ref,
-    vb, sv, lhs, vh, vl, th, tl, ys, yr, sb, rbuf, ob, rb, xs, cx, gp, sxp, cxs, cxr, cys, cyr,
-    d_ref, p1_ref, ie_ref,
-    a_send, a_recv, h_send, h_recv, l_sem,
+    vb, adv, cot, vm_ref, vt_ref, large,
+    sv, lhs, vh, vl, th, tl, ys, yr, sb, rbuf, ob, rb, gp, sxp, cxs, cxr, cys, cyr,
+    p1_ref, ie_ref,
+    a_send, a_recv, h_send, h_recv, l_sem, all_sem,
 ):
     gx, gy = lax.axis_index("gx"), lax.axis_index("gy")
     me = gx * GY + gy
     left_x, right_x = lax.rem(gx + GX - 1, GX), lax.rem(gx + 1, GX)
     left_y, right_y = lax.rem(gy + GY - 1, GY), lax.rem(gy + 1, GY)
 
-    def other(i):
-        t = lax.rem(me + i, DEVICES)
-        return t, lax.div(t, GY), lax.rem(t, GY)
-
+    parity, owner = lax.rem(gy, 2), gx * 8 + lax.div(gy, 2)
     barrier = pltpu.get_barrier_semaphore()
-
-    def greet(i, carry):
-        _, tx, ty = other(i)
-        pl.semaphore_signal(barrier, inc=1, device_id=(tx, ty), device_id_type=MESH)
-        return carry
-
-    lax.fori_loop(1, DEVICES, greet, 0)
+    for i in range(1, GX):
+        pl.semaphore_signal(barrier, inc=1, device_id=(lax.rem(gx + i, GX), gy), device_id_type=MESH)
+    for i in range(1, GY):
+        pl.semaphore_signal(barrier, inc=1, device_id=(gx, lax.rem(gy + i, GY)), device_id_type=MESH)
+
+    loads = [
+        pltpu.make_async_copy(source, target, l_sem.at[n])
+        for n, (source, target) in enumerate(
+            (
+                (vel_h, vb.at[:, pl.ds(2, BX), pl.ds(8, BY)]),
+                (vm_h, vm_ref),
+                (vt_h, vt_ref),
+                (cot_h, cot),
+                (adv_h, adv),
+                (large_h, large),
+            )
+        )
+    ]
+    for load in loads:
+        load.start()
+    loads[0].wait()
 
     for c in range(3):
         for x in range(BX):
-            ys[0, c, 2 * x : 2 * x + 2, :] = vel[c, x, 0:2, :]
-            ys[1, c, 2 * x : 2 * x + 2, :] = vel[c, x, BY - 2 : BY, :]
-
-    pl.semaphore_wait(barrier, DEVICES - 1)
+            ys[0, c, 2 * x : 2 * x + 2, :] = vb[c, x + 2, 8:10, :]
+            ys[1, c, 2 * x : 2 * x + 2, :] = vb[c, x + 2, 6 + BY : 8 + BY, :]
+
+    pl.semaphore_wait(barrier, GX + GY - 2)
 
     def remote(src, dst, n, x, y):
         return pltpu.make_async_remote_copy(
@@ -176,16 +208,19 @@
         )
 
     halo = [
-        remote(vel.at[:, pl.ds(0, 2)], vb.at[:, pl.ds(BX + 2, 2), pl.ds(8, BY)], 0, left_x, gy),
-        remote(vel.at[:, pl.ds(BX - 2, 2)], vb.at[:, pl.ds(0, 2), pl.ds(8, BY)], 1, right_x, gy),
+        remote(vel_h.at[:, pl.ds(0, 2)], vb.at[:, pl.ds(BX + 2, 2), pl.ds(8, BY)], 0, left_x, gy),
+        remote(vel_h.at[:, pl.ds(BX - 2, 2)], vb.at[:, pl.ds(0, 2), pl.ds(8, BY)], 1, right_x, gy),
         remote(ys.at[0], yr.at[1], 2, gx, left_y),
         remote(ys.at[1], yr.at[0], 3, gx, right_y),
     ]
     for copy in halo:
         copy.start()
 
-    for c in range(3):
-        vb[c, 2 : BX + 2, 8 : 8 + BY, :] = vel[c]
+    for i in range(1, GY):
+        pl.semaphore_signal(all_sem, inc=1, device_id=(gx, lax.rem(gy + i, GY)), device_id_type=MESH)
+
+    loads[1].wait()
+    loads[2].wait()
     for full, high, low in ((vm_ref, vh, vl), (vt_ref, th, tl)):
         for i in range(0, NZ, 64):
             h, l = halves(full[i : i + 64, :])
@@ -235,12 +270,53 @@
             jnp.concatenate([w[1], d_parts[1]], axis=0),
         )
         s = dot3((ts_h[...], ts_l[...]), both)
-        d_ref[group * SLOTS : group * SLOTS + 64, :] = s
-        d_ref[group * SLOTS + 16 : group * SLOTS + 32, :] += wide_rows[128:144]
-        d_ref[group * SLOTS + 40 : group * SLOTS + 48, :] += wide_rows[144:152]
-
+        some, few = jnp.zeros((16, NZ), f32), jnp.zeros((8, NZ), f32)
+        s = s + jnp.concatenate([some, wide_rows[128:144], few, wide_rows[144:152], some], axis=0)
+        s = jnp.concatenate([s[:, : NZ // 2], s[:, NZ // 2 :]], axis=0)
+        for i in range(2):
+            sb[group, 128 * i : 128 * i + 128, :] = s[:, 128 * i : 128 * i + 128].T
+
+    def chunk(n):
+        return pl.ds(n * OWNED, OWNED)
+
+    place = gy * GX + gx
+
+    def to_owners(group):
+        def copy_to(k):
+            t = lax.rem(owner + k, OWNERS)
+            return pltpu.make_async_remote_copy(
+                src_ref=sb.at[group, chunk(t)], dst_ref=rbuf.at[chunk(place)],
+                send_sem=a_send.at[group], recv_sem=a_recv.at[0],
+                device_id=(lax.div(t, 8), lax.rem(t, 8) * 2 + group), device_id_type=MESH,
+            )
+
+        @pl.when(parity != group)
+        def _():
+            copy_to(0).start()
+
+        @pl.when(parity == group)
+        def _():
+            pltpu.make_async_copy(sb.at[group, chunk(owner)], rbuf.at[chunk(place)], a_recv.at[0]).start()
+
+        def start(k, carry):
+            copy_to(k).start()
+            return carry
+
+        lax.fori_loop(1, OWNERS, start, 0)
+
+    def span(ref, chunks, send, recv):
+        rows = ref.at[pl.ds(0, chunks * OWNED)]
+        return pltpu.make_async_remote_copy(
+            src_ref=rows, dst_ref=rows, send_sem=a_send.at[send], recv_sem=a_recv.at[recv],
+            device_id=(right_x, gy), device_id_type=MESH,
+        )
+
+    loads[3].wait()
     forward(1, cot)
-
+    pl.semaphore_wait(all_sem, GY - 1)
+    to_owners(1)
+
+    loads[4].wait()
     for copy in halo:
         copy.wait()
     for c in range(3):
@@ -264,77 +340,65 @@
     lax.fori_loop(0, BX, section_row, 0)
     forward(0, sv)
 
-    for i in range(4):
-        sb[128 * i : 128 * i + 128, :] = d_ref[:, 128 * i : 128 * i + 128].T
-
-    def exchange(n, src, dst, src_row, dst_row):
-        def start(i, carry):
-            t, tx, ty = other(i)
-            pltpu.make_async_remote_copy(
-                src_ref=src.at[pl.ds(src_row(t, tx, ty) * OWNED, OWNED)],
-                dst_ref=dst.at[pl.ds(dst_row * OWNED, OWNED)],
-                send_sem=a_send.at[n], recv_sem=a_recv.at[n],
-                device_id=(tx, ty), device_id_type=MESH,
-            ).start()
-            return carry
-
-        lax.fori_loop(1, DEVICES, start, 0)
-        local = pltpu.make_async_copy(
-            src.at[pl.ds(src_row(me, gx, gy) * OWNED, OWNED)],
-            dst.at[pl.ds(dst_row * OWNED, OWNED)],
-            l_sem.at[n],
-        )
-        local.start()
-        local.wait()
-        whole = pltpu.make_async_remote_copy(
-            src_ref=src.at[pl.ds(0, (DEVICES - 1) * OWNED)],
-            dst_ref=dst.at[pl.ds(0, (DEVICES - 1) * OWNED)],
-            send_sem=a_send.at[n], recv_sem=a_recv.at[n],
-            device_id=(right_x, gy), device_id_type=MESH,
-        )
-        whole.wait_send()
-        whole.wait_recv()
-
-    place = gy * GX + gx
-    exchange(0, sb, rbuf, lambda t, tx, ty: t, place)
-
-    low_lanes = lax.broadcasted_iota(jnp.int32, (32, 128), 1) < SLOTS
-    for pair in range(GY // 2):
-        a = rbuf[64 * pair : 64 * pair + 32, :]
-        b = rbuf[64 * pair + 32 : 64 * pair + 64, :]
-        xs[0:32, 128 * pair : 128 * pair + 128] = jnp.where(low_lanes, a, pltpu.roll(b, 64, 1))
-        xs[32:64, 128 * pair : 128 * pair + 128] = jnp.where(low_lanes, pltpu.roll(a, 64, 1), b)
-    y1 = dot3(halves(xs[...]), (w1_h[...], w1_l[...]))
-    stacked = jnp.concatenate([y1[:, 0:256], y1[:, 256:512]], axis=0)
-    for x in range(BX):
-        cx[64 * x : 64 * x + 64, :] = y1[:, 512 + 32 * x : 544 + 32 * x]
-    hat = dot3((rw_h[...], rw_l[...]), halves(stacked))
-    inner = dot3((cl_h[...], cl_l[...]), halves(cx[...]))
-    hat = hat + dot3(halves(inner), (wc_h[...], wc_l[...]))
-    row_mode = lax.rem(lax.broadcasted_iota(jnp.int32, (512, 128), 0), OWNED)
+    to_owners(0)
+
+    loads[5].wait()
+    span(rbuf, DEVICES, 0, 0).wait_recv()
+    sides = [
+        regroup([rbuf[32 * (8 * half + i) : 32 * (8 * half + i) + 32, :] for i in range(8)])
+        for half in range(2)
+    ]
+    rows = [jnp.concatenate([sides[0][j], sides[1][j]], axis=1) for j in range(8)]
+    along = dot3(halves(jnp.concatenate([rows[0], rows[4], rows[1], rows[5]], axis=0)), (qy_h[...], qy_l[...]))
+    columns = halves(jnp.concatenate([rows[2], rows[6]], axis=0))
+    columns = dot(columns[0], order_ref[...]) + dot(columns[1], order_ref[...])
+    columns = jnp.concatenate([columns[:, 32 * x : 32 * x + 32] for x in range(BX)], axis=0)
+    inner = halves(dot_narrow((large[0], large[1]), halves(columns)))
+    along = halves(along)
+    left = (
+        jnp.concatenate([rw_h[...], inner[0]], axis=1),
+        jnp.concatenate([rw_l[...], inner[1]], axis=1),
+    )
+    right = (
+        jnp.concatenate([along[0], wc_h[...]], axis=0),
+        jnp.concatenate([along[1], wc_l[...]], axis=0),
+    )
+    hat = dot3(left, right)
+    row = lax.broadcasted_iota(jnp.int32, (512, 128), 0)
+    row_mode = lax.rem(row, OWNED) + OWNED * lax.div(row, 256)
     rate = jnp.zeros((512, 128), f32)
-    for m in range(OWNED):
-        rate = jnp.where(row_mode == m, rate_s[me * OWNED + m], rate)
-    hat = hat / (wide(rate + lamx_ref[...], 256) + lamy_ref[...])
-    hat_parts = halves(hat)
-    back = dot3((rt_h[...], rt_l[...]), hat_parts)
-    inner = dot3(hat_parts, (wt_h[...], wt_l[...]))
-    cx[...] = dot3((ct_h[...], ct_l[...]), halves(inner))
-    parts = [back[0:64], back[64:128]] + [cx[64 * x : 64 * x + 64, :] for x in range(BX)]
-    xs[...] = dot3(halves(jnp.concatenate(parts, axis=1)), (w1_h[...], w1_l[...]), nt=True)
-    for pair in range(GY // 2):
-        p = xs[0:32, 128 * pair : 128 * pair + 128]
-        q = xs[32:64, 128 * pair : 128 * pair + 128]
-        ob[64 * pair : 64 * pair + 32, :] = jnp.where(low_lanes, p, pltpu.roll(q, 64, 1))
-        ob[64 * pair + 32 : 64 * pair + 64, :] = jnp.where(low_lanes, pltpu.roll(p, 64, 1), q)
-
-    exchange(1, ob, rb, lambda t, tx, ty: ty * GX + tx, me)
-
-    for i in range(4):
-        d_ref[:, 128 * i : 128 * i + 128] = rb[128 * i : 128 * i + 128, :].T
+    for m in range(2 * OWNED):
+        one = rate_s[owner * OWNED + m % OWNED + (NZ // 2) * (m // OWNED)]
+        rate = jnp.where(row_mode == m, one, rate)
+    hat = halves(hat / (wide(rate + lamx_ref[...], 256) + lamy_ref[...]))
+    along = dot3(halves(dot3((rt_h[...], rt_l[...]), hat)), (qt_h[...], qt_l[...]))
+    columns = dot_narrow((large[2], large[3]), halves(dot3(hat, (wt_h[...], wt_l[...]))))
+    columns = halves(jnp.concatenate([columns[64 * x : 64 * x + 64, :] for x in range(BX)], axis=1))
+    columns = dot(columns[0], ordert_ref[...]) + dot(columns[1], ordert_ref[...])
+    nothing = jnp.zeros((32, 256), f32)
+    rows = [along[0:32], along[64:96], columns[0:32], nothing, along[32:64], along[96:128], columns[32:64], nothing]
+    for half in range(2):
+        for i, block in enumerate(regroup([r[:, 128 * half : 128 * half + 128] for r in rows])):
+            ob[32 * (8 * half + i) : 32 * (8 * half + i) + 32, :] = block
+
+    pltpu.make_async_copy(ob.at[chunk(place)], rb.at[parity, chunk(owner)], a_recv.at[1 + parity]).start()
+
+    def answer(i, carry):
+        t = lax.rem(gx * GY + gy + i, DEVICES)
+        tx, ty = lax.div(t, GY), lax.rem(t, GY)
+        pltpu.make_async_remote_copy(
+            src_ref=ob.at[chunk(ty * GX + tx)], dst_ref=rb.at[parity, chunk(owner)],
+            send_sem=a_send.at[2], recv_sem=a_recv.at[1 + parity],
+            device_id=(tx, ty), device_id_type=MESH,
+        ).start()
+        return carry
+
+    lax.fori_loop(1, DEVICES, answer, 0)
 
     def backward(group):
-        u = d_ref[group * SLOTS : group * SLOTS + SLOTS, :]
+        span(rb.at[group], OWNERS, 0, 1 + group).wait_recv()
+        u = jnp.concatenate([rb[group, 0:128, :].T, rb[group, 128:256, :].T], axis=1)
+        u = jnp.concatenate([u[0:SLOTS], u[SLOTS:]], axis=1)
         u_parts = halves(u)
         inside = (p1_ref[group] + dot3((nt_h[...], nt_l[...]), u_parts)) * ie_ref[...]
         in_parts = halves(inside)
@@ -396,13 +460,6 @@
     for copy in edges:
         copy.start()
 
-    tilted = backward(0)
-    for x in range(BX):
-        c0, c1 = corrections(0, x)
-        next_ref[0, x] = sv[0, x] - c0
-        next_ref[1, x] = sv[1, x] - c1
-        next_ref[2, x] = sv[2, x] - tilted[BY * x : BY * x + BY]
-
     def adjoint_row(x, carry):
         kx = {}
         for offset in (-2, -1, 0, 1, 2):
@@ -419,6 +476,14 @@
         return carry
 
     lax.fori_loop(0, BX, adjoint_row, 0)
+
+    tilted = backward(0)
+    for x in range(BX):
+        c0, c1 = corrections(0, x)
+        next_ref[0, x] = sv[0, x] - c0
+        next_ref[1, x] = sv[1, x] - c1
+        next_ref[2, x] = sv[2, x] - tilted[BY * x : BY * x + BY]
+
     for copy in edges:
         copy.wait()
     for c in range(3):
@@ -429,6 +494,17 @@
             adj_ref[c, x, 0:2, :] += scale * cyr[0, c, 2 * x : 2 * x + 2, :]
             adj_ref[c, x, BY - 2 : BY, :] += scale * cyr[1, c, 2 * x : 2 * x + 2, :]
 
+    span(rbuf, DEVICES - 1, 2, 0).wait_send()
+    for group in range(2):
+
+        @pl.when(parity != group)
+        def _():
+            span(rbuf, OWNERS, group, 0).wait_send()
+
+        @pl.when(parity == group)
+        def _():
+            span(rbuf, OWNERS - 1, group, 0).wait_send()
+
 
 def per_device(
     velocity_now, advecting, cotangent, building_height, section_index,
@@ -437,14 +513,20 @@
     constants = tables()
     vmem = pl.BlockSpec(memory_space=pltpu.VMEM)
     smem = pl.BlockSpec(memory_space=pltpu.SMEM)
+    hbm = pl.BlockSpec(memory_space=pl.ANY)
     field = jax.ShapeDtypeStruct((3, BX, BY, NZ), f32)
     return pl.pallas_call(
         kernel,
         out_shape=(field, field),
-        in_specs=[vmem, vmem, vmem, vmem, smem, vmem, vmem, vmem, smem] + [vmem] * len(constants),
+        in_specs=[hbm, hbm, hbm, vmem, smem, hbm, hbm, vmem, smem, hbm] + [vmem] * (len(constants) - 1),
         out_specs=(vmem, vmem),
         scratch_shapes=[
             pltpu.VMEM((3, BX + 4, 32, NZ), f32),
+            pltpu.VMEM((3, BX, BY, NZ), f32),
+            pltpu.VMEM((3, BX, BY, NZ), f32),
+            pltpu.VMEM((NZ, NZ), f32),
+            pltpu.VMEM((NZ, NZ), f32),
+            pltpu.VMEM((4, 512, 512), bf16),
             pltpu.VMEM((3, BX, BY, NZ), f32),
             pltpu.VMEM((2, 160, NZ), f32),
             pltpu.VMEM((NZ, NZ), bf16),
@@ -453,26 +535,24 @@
             pltpu.VMEM((NZ, NZ), bf16),
             pltpu.VMEM((2, 3, 16, NZ), f32),
             pltpu.VMEM((2, 3, 16, NZ), f32),
+            pltpu.VMEM((2, NZ // 2, 128), f32),
             pltpu.VMEM((NZ, 128), f32),
             pltpu.VMEM((NZ, 128), f32),
-            pltpu.VMEM((NZ, 128), f32),
-            pltpu.VMEM((NZ, 128), f32),
-            pltpu.VMEM((64, 1024), f32),
-            pltpu.VMEM((512, 32), f32),
+            pltpu.VMEM((2, NZ // 2, 128), f32),
             pltpu.VMEM((3, BX + 4, BY, NZ), f32),
             pltpu.VMEM((BX + 4, BY, NZ), f32),
             pltpu.VMEM((2, 3, 2, BY, NZ), f32),
             pltpu.VMEM((2, 3, 2, BY, NZ), f32),
             pltpu.VMEM((2, 3, 16, NZ), f32),
             pltpu.VMEM((2, 3, 16, NZ), f32),
-            pltpu.VMEM((128, NZ), f32),
             pltpu.VMEM((2, 128, NZ), f32),
             pltpu.VMEM((128, NZ), f32),
-            pltpu.SemaphoreType.DMA((2,)),
-            pltpu.SemaphoreType.DMA((2,)),
+            pltpu.SemaphoreType.DMA((3,)),
+            pltpu.SemaphoreType.DMA((3,)),
             pltpu.SemaphoreType.DMA((8,)),
             pltpu.SemaphoreType.DMA((8,)),
-            pltpu.SemaphoreType.DMA((2,)),
+            pltpu.SemaphoreType.DMA((6,)),
+            pltpu.SemaphoreType.REGULAR,
         ],
         compiler_params=pltpu.CompilerParams(
             collective_id=0, has_side_effects=True, vmem_limit_bytes=56 * 1024 * 1024

time: 65.6 us -> 52.2 us (0.80)
  Pallas kernels: 61.2 us -> 47.7 us
    pallas_call x1, Pallas kernels: 61.2 us -> 47.7 us  [per_device(): pl.pallas_call(kernel, out_shape=(field, field), in_specs=[hbm, hbm, hbm,...]
where the time goes in v2:
time: 52.2 us; the launch traced here: 52.1 us
  Pallas kernels  47.7 us (91%)
  local copies, waits for them, and re-layouts  3.04 us (6%)
  between operations  1.29 us (2%)
    pallas_call x1, Pallas kernels, per_device(): pl.pallas_call(kernel, out_shape=(field, field), in_specs=[hbm, hbm, hbm,...  47.7 us
    unnamed x4, local copies, waits for them, and re-layouts  3.04 us

profile of v2, /device:TPU:1, one launch (start us, length us, event | category | flops | bytes accessed | tf_op | source)
XLA Modules:
  0.0 52.1 jit_solution(3127583138304662101)
XLA Ops:
  1.3 47.7 %shard_map.329 = (f32[3,8,16,512]{3,2,1,0:T(8,128)}, f32[3,8,16,512]{3,2,1,0:T(8,128)}) custom-call(f32[3,8,16,512]{3,2,1,0:T(8,128)} %vel_h.1, f32[3,8,16,512]{3,2,1,0:T(8,128)} %adv_h.1, f32[3,8,16,512]{3,2,1,0:T(8,128)} %cot_h.1, s32[8,16]{1,0:T(8,128)} %height.1, s32[1]{0:T(128)S(6)} %copy.38.section, f32[512,512]{1,0:T(8,128)} %vm_h.1, ...), custom_call_target="tpu_custom_call" | custom-call | tf_op jit(solution)/shard_map/pallas_call | solution.py:518
  49.0 0.0 copy-start
  49.0 2.2 %copy.39 = f32[3,8,16,512]{3,2,1,0:T(8,128)} copy(f32[3,8,16,512]{3,2,1,0:T(8,128)} %get-tuple-element.4) | data formatting | bytes 1572864
  51.2 0.0 copy-done
  51.2 0.9 %copy.40 = f32[3,8,16,512]{3,2,1,0:T(8,128)} copy(f32[3,8,16,512]{3,2,1,0:T(8,128)S(1)} %copy-done) | data formatting | bytes 1572864
Async XLA Ops:
  49.0 2.2 %copy-start = (f32[3,8,16,512]{3,2,1,0:T(8,128)S(1)}, f32[3,8,16,512]{3,2,1,0:T(8,128)}, u32[]{:S(2)}) copy-start(f32[3,8,16,512]{3,2,1,0:T(8,128)} %get-tuple-element.5) | copy-start | bytes 2359300

commit v3 on v2

--- a/solution.py
+++ b/solution.py
@@ -18,6 +18,7 @@
 OWNERS = DEVICES // 2
 OWNED = NZ // OWNERS // 2
 SLOTS = 64
+LARGE, MID, NARROW = 2304, 992, 688
 f32, bf16 = jnp.float32, jnp.bfloat16
 
 
@@ -36,10 +37,12 @@
     return basis, freq
 
 
-def split_const(matrix):
-    high = matrix.astype(ml_dtypes.bfloat16)
-    low = (matrix - high.astype(np.float64)).astype(ml_dtypes.bfloat16)
-    return high, low
+def split_const(matrix, count=2):
+    parts = []
+    for _ in range(count):
+        parts.append(matrix.astype(ml_dtypes.bfloat16))
+        matrix = matrix - parts[-1].astype(np.float64)
+    return parts
 
 
 def tables():
@@ -49,7 +52,6 @@
     sin_x[0], sin_x[:, 0], sin_y[0], sin_y[:, 0] = 0.0, 0.0, 0.0, 0.0
     sine = np.kron(sin_x, sin_y)
     mu = (2.0 - 2.0 * np.cos(math.pi * j / BX))[:, None] + (2.0 - 2.0 * np.cos(math.pi * k / BY))
-    mu = np.repeat(mu.reshape(-1, 1), 128, axis=1)
     near = np.zeros((SLOTS, BX * BY))
     own = np.zeros((SLOTS, BX * BY))
     for y in range(BY):
@@ -83,16 +85,39 @@
     rows = rows.reshape(512, 128)
     cols = cols.reshape(512, 512)
     wc = np.stack([qy[0::16], np.roll(qy[0::16], -1, axis=0)]).reshape(32, 256)
-    lam_x = np.repeat(np.broadcast_to(lx[None, :, None], (2, NX, OWNED)).reshape(512, 1), 128, axis=1)
-    lam_y = ly[None, :]
-    out = []
-    for matrix in [sine, to_slots, near.T, from_slots, qy, qy.T, rows, rows.T, wc, wc.T]:
-        out.extend(split_const(np.ascontiguousarray(matrix)))
-    for matrix in [order, order.T]:
-        out.append(matrix.astype(ml_dtypes.bfloat16))
-    large = np.stack(split_const(cols) + split_const(cols.T))
-    plain = [mu.astype(np.float32), lam_x.astype(np.float32), lam_y.astype(np.float32)]
-    return [jnp.asarray(t) for t in [large] + out + plain]
+    lam_x = np.broadcast_to(lx[None, :, None], (2, NX, OWNED)).reshape(512)
+
+    def columns(values):
+        out = np.zeros((values.size, 128), ml_dtypes.bfloat16)
+        for n, part in enumerate(split_const(values.reshape(-1), 3)):
+            out[:, n] = part
+        return out
+
+    def packed(matrices, lanes):
+        parts = []
+        for matrix in matrices:
+            for part in split_const(np.ascontiguousarray(matrix)):
+                parts.append(np.pad(part, ((0, 0), (0, lanes - part.shape[1]))))
+        return np.concatenate(parts)
+
+    exact = np.concatenate([order, order.T]).astype(ml_dtypes.bfloat16)
+    lam_y = np.stack(split_const(ly, 3)).reshape(6, 128)
+    large = packed([cols, cols.T, rows.T], 512)
+    mid = np.concatenate([exact, packed([qy, qy.T, wc, to_slots, from_slots], 256)])
+    narrow = np.concatenate([packed([sine, rows, near.T, wc.T], 128), columns(lam_x), columns(mu), lam_y])
+    narrow = np.pad(narrow, ((0, 4 * NARROW - narrow.shape[0]), (0, 0)))
+    mid = np.concatenate([mid[:MID], mid[MID:]], axis=1)
+    narrow = np.concatenate([narrow[NARROW * i : NARROW * i + NARROW] for i in range(4)], axis=1)
+    return jnp.asarray(np.concatenate([large, mid, narrow]))
+
+
+def summed(parts):
+    parts = parts.astype(f32)
+    return parts[:, 0:1] + (parts[:, 1:2] + parts[:, 2:3])
+
+
+def unpacked(ref, start, rows, lanes):
+    return ref[start : start + rows, :lanes], ref[start + rows : start + 2 * rows, :lanes]
 
 
 def halves(value):
@@ -156,11 +181,9 @@
 
 
 def kernel(
-    vel_h, adv_h, cot_h, height, section, vm_h, vt_h, rate_row, rate_s, large_h,
-    sine_h, sine_l, ts_h, ts_l, nt_h, nt_l, fs_h, fs_l, qy_h, qy_l, qt_h, qt_l, rw_h, rw_l, rt_h, rt_l,
-    wc_h, wc_l, wt_h, wt_l, order_ref, ordert_ref, mu_ref, lamx_ref, lamy_ref,
+    vel_h, adv_h, cot_h, small, vm_h, vt_h, tables_h,
     next_ref, adj_ref,
-    vb, adv, cot, vm_ref, vt_ref, large,
+    vb, adv, cot, vm_ref, vt_ref, large, mid, narrow,
     sv, lhs, vh, vl, th, tl, ys, yr, sb, rbuf, ob, rb, gp, sxp, cxs, cxr, cys, cyr,
     p1_ref, ie_ref,
     a_send, a_recv, h_send, h_recv, l_sem, all_sem,
@@ -170,7 +193,8 @@
     left_x, right_x = lax.rem(gx + GX - 1, GX), lax.rem(gx + 1, GX)
     left_y, right_y = lax.rem(gy + GY - 1, GY), lax.rem(gy + 1, GY)
 
-    parity, owner = lax.rem(gy, 2), gx * 8 + lax.div(gy, 2)
+    parity, half_y = lax.rem(gy, 2), lax.div(gy, 2)
+    owner = gx * 8 + half_y
     barrier = pltpu.get_barrier_semaphore()
     for i in range(1, GX):
         pl.semaphore_signal(barrier, inc=1, device_id=(lax.rem(gx + i, GX), gy), device_id_type=MESH)
@@ -186,12 +210,20 @@
                 (vt_h, vt_ref),
                 (cot_h, cot),
                 (adv_h, adv),
-                (large_h, large),
+                (tables_h.at[pl.ds(0, LARGE)], large),
+            )
+            + tuple(
+                (tables_h.at[pl.ds(LARGE + MID, NARROW), pl.ds(128 * i, 128)], narrow.at[pl.ds(NARROW * i, NARROW)])
+                for i in range(4)
+            )
+            + tuple(
+                (tables_h.at[pl.ds(LARGE, MID), pl.ds(256 * i, 256)], mid.at[pl.ds(MID * i, MID)])
+                for i in range(2)
             )
         )
     ]
-    for load in loads:
-        load.start()
+    for n in (0, 3, 1, 2, 6, 7, 8, 9, 10, 11, 4, 5):
+        loads[n].start()
     loads[0].wait()
 
     for c in range(3):
@@ -213,8 +245,8 @@
         remote(ys.at[0], yr.at[1], 2, gx, left_y),
         remote(ys.at[1], yr.at[0], 3, gx, right_y),
     ]
-    for copy in halo:
-        copy.start()
+    for n in (2, 3, 0, 1):
+        halo[n].start()
 
     for i in range(1, GY):
         pl.semaphore_signal(all_sem, inc=1, device_id=(gx, lax.rem(gy + i, GY)), device_id_type=MESH)
@@ -226,13 +258,12 @@
             h, l = halves(full[i : i + 64, :])
             high[i : i + 64, :] = h
             low[i : i + 64, :] = l
-    ie_ref[...] = 1.0 / (wide(mu_ref[...], NZ) + rate_row[...])
-
-    number = section[0]
-    part = lax.rem(number, 3)
-    step = lax.div(number, 3).astype(f32)
-    fraction = jnp.where(part == 0, f32(1.0 / 3.0), jnp.where(part == 1, f32(0.5), f32(1.0)))
-    factor = (f32(0.2) + step * f32(0.2 / 63.0)) * fraction
+    for n in range(6, 10):
+        loads[n].wait()
+    rate_row = jnp.concatenate([small[n : n + 1, :] for n in range(4)], axis=1)
+    ie_ref[...] = 1.0 / (summed(narrow[2560:2688, :]) + rate_row)
+
+    factor = small[4:5, 0:1]
     scale = factor * f32(-1.0 / 12.0)
 
     levels = lax.broadcasted_iota(jnp.int32, (BY, NZ), 1).astype(f32)
@@ -241,7 +272,7 @@
     )
 
     def fluid_at(x):
-        row = height[pl.ds(x, 1), :].astype(f32)
+        row = small[pl.ds(8 + x, 1), 0:BY]
         column = jnp.sum(jnp.where(diagonal, row, 0.0), axis=1, keepdims=True)
         return (levels >= column).astype(f32)
 
@@ -262,14 +293,14 @@
         tilted = dot3(halves(field[2].reshape(BX * BY, NZ)), (th[...], tl[...]))
         d = wide_rows[:128] + tilted
         d_parts = halves(d)
-        p1 = dot3((sine_h[...], sine_l[...]), d_parts)
+        p1 = dot3(unpacked(narrow, 0, 128, 128), d_parts)
         p1_ref[group] = p1
         w = halves(p1 * ie_ref[...])
         both = (
             jnp.concatenate([w[0], d_parts[0]], axis=0),
             jnp.concatenate([w[1], d_parts[1]], axis=0),
         )
-        s = dot3((ts_h[...], ts_l[...]), both)
+        s = dot3(unpacked(mid, 1600, 64, 256), both)
         some, few = jnp.zeros((16, NZ), f32), jnp.zeros((8, NZ), f32)
         s = s + jnp.concatenate([some, wide_rows[128:144], few, wide_rows[144:152], some], axis=0)
         s = jnp.concatenate([s[:, : NZ // 2], s[:, NZ // 2 :]], axis=0)
@@ -282,27 +313,30 @@
     place = gy * GX + gx
 
     def to_owners(group):
-        def copy_to(k):
-            t = lax.rem(owner + k, OWNERS)
+        def copy_to(dx, dy):
+            tx, ty = lax.rem(gx + dx, GX), lax.rem(half_y + dy, 8)
             return pltpu.make_async_remote_copy(
-                src_ref=sb.at[group, chunk(t)], dst_ref=rbuf.at[chunk(place)],
+                src_ref=sb.at[group, chunk(tx * 8 + ty)], dst_ref=rbuf.at[chunk(place)],
                 send_sem=a_send.at[group], recv_sem=a_recv.at[0],
-                device_id=(lax.div(t, 8), lax.rem(t, 8) * 2 + group), device_id_type=MESH,
+                device_id=(tx, ty * 2 + group), device_id_type=MESH,
             )
 
         @pl.when(parity != group)
         def _():
-            copy_to(0).start()
+            copy_to(0, 0).start()
 
         @pl.when(parity == group)
         def _():
             pltpu.make_async_copy(sb.at[group, chunk(owner)], rbuf.at[chunk(place)], a_recv.at[0]).start()
 
-        def start(k, carry):
-            copy_to(k).start()
+        def start(dx, carry):
+            for dy in range(8):
+                copy_to(dx, dy).start()
             return carry
 
-        lax.fori_loop(1, OWNERS, start, 0)
+        for dy in range(1, 8):
+            copy_to(0, dy).start()
+        lax.fori_loop(1, GX, start, 0)
 
     def span(ref, chunks, send, recv):
         rows = ref.at[pl.ds(0, chunks * OWNED)]
@@ -312,13 +346,15 @@
         )
 
     loads[3].wait()
+    loads[10].wait()
+    loads[11].wait()
     forward(1, cot)
     pl.semaphore_wait(all_sem, GY - 1)
     to_owners(1)
 
     loads[4].wait()
-    for copy in halo:
-        copy.wait()
+    halo[2].wait()
+    halo[3].wait()
     for c in range(3):
         for x in range(BX):
             vb[c, x + 2, 6:8, :] = yr[0, c, 2 * x : 2 * x + 2, :]
@@ -337,7 +373,11 @@
             sv[c, x] = fluid * (center + scale * total)
         return carry
 
-    lax.fori_loop(0, BX, section_row, 0)
+    lax.fori_loop(2, BX - 2, section_row, 0)
+    halo[0].wait()
+    halo[1].wait()
+    lax.fori_loop(0, 2, section_row, 0)
+    lax.fori_loop(BX - 2, BX, section_row, 0)
     forward(0, sv)
 
     to_owners(0)
@@ -349,32 +389,34 @@
         for half in range(2)
     ]
     rows = [jnp.concatenate([sides[0][j], sides[1][j]], axis=1) for j in range(8)]
-    along = dot3(halves(jnp.concatenate([rows[0], rows[4], rows[1], rows[5]], axis=0)), (qy_h[...], qy_l[...]))
+    along = dot3(halves(jnp.concatenate([rows[0], rows[4], rows[1], rows[5]], axis=0)), unpacked(mid, 512, 256, 256))
     columns = halves(jnp.concatenate([rows[2], rows[6]], axis=0))
-    columns = dot(columns[0], order_ref[...]) + dot(columns[1], order_ref[...])
+    columns = dot(columns[0], mid[0:256, :]) + dot(columns[1], mid[0:256, :])
     columns = jnp.concatenate([columns[:, 32 * x : 32 * x + 32] for x in range(BX)], axis=0)
-    inner = halves(dot_narrow((large[0], large[1]), halves(columns)))
+    inner = halves(dot_narrow(unpacked(large, 0, 512, 512), halves(columns)))
     along = halves(along)
-    left = (
-        jnp.concatenate([rw_h[...], inner[0]], axis=1),
-        jnp.concatenate([rw_l[...], inner[1]], axis=1),
-    )
-    right = (
-        jnp.concatenate([along[0], wc_h[...]], axis=0),
-        jnp.concatenate([along[1], wc_l[...]], axis=0),
-    )
+    row_table, edge_table = unpacked(narrow, 256, 512, 128), unpacked(mid, 1536, 32, 256)
+    left = [jnp.concatenate([row_table[i], inner[i]], axis=1) for i in range(2)]
+    right = [jnp.concatenate([along[i], edge_table[i]], axis=0) for i in range(2)]
     hat = dot3(left, right)
     row = lax.broadcasted_iota(jnp.int32, (512, 128), 0)
     row_mode = lax.rem(row, OWNED) + OWNED * lax.div(row, 256)
     rate = jnp.zeros((512, 128), f32)
-    for m in range(2 * OWNED):
-        one = rate_s[owner * OWNED + m % OWNED + (NZ // 2) * (m // OWNED)]
-        rate = jnp.where(row_mode == m, one, rate)
-    hat = halves(hat / (wide(rate + lamx_ref[...], 256) + lamy_ref[...]))
-    along = dot3(halves(dot3((rt_h[...], rt_l[...]), hat)), (qt_h[...], qt_l[...]))
-    columns = dot_narrow((large[2], large[3]), halves(dot3(hat, (wt_h[...], wt_l[...]))))
+    lane = lax.broadcasted_iota(jnp.int32, (1, 128), 1)
+    first_lane = lax.rem(owner, 128 // OWNED) * OWNED
+    for half in range(2):
+        rates = small[pl.ds(2 * half + lax.div(owner, 128 // OWNED), 1), :]
+        for m in range(OWNED):
+            one = jnp.sum(jnp.where(lane == first_lane + m, rates, 0.0), axis=1, keepdims=True)
+            rate = jnp.where(row_mode == OWNED * half + m, one, rate)
+    lam_y = narrow[2688:2704, :].astype(f32)
+    lam_y = [lam_y[n : n + 1] + (lam_y[n + 2 : n + 3] + lam_y[n + 4 : n + 5]) for n in range(2)]
+    lam_y = jnp.concatenate(lam_y, axis=1)
+    hat = halves(hat / (wide(rate + summed(narrow[2048:2560, :]), 256) + lam_y))
+    along = dot3(halves(dot3(unpacked(large, 2048, 128, 512), hat)), unpacked(mid, 1024, 256, 256))
+    columns = dot_narrow(unpacked(large, 1024, 512, 512), halves(dot3(hat, unpacked(narrow, 1536, 256, 32))))
     columns = halves(jnp.concatenate([columns[64 * x : 64 * x + 64, :] for x in range(BX)], axis=1))
-    columns = dot(columns[0], ordert_ref[...]) + dot(columns[1], ordert_ref[...])
+    columns = dot(columns[0], mid[256:512, :]) + dot(columns[1], mid[256:512, :])
     nothing = jnp.zeros((32, 256), f32)
     rows = [along[0:32], along[64:96], columns[0:32], nothing, along[32:64], along[96:128], columns[32:64], nothing]
     for half in range(2):
@@ -383,30 +425,35 @@
 
     pltpu.make_async_copy(ob.at[chunk(place)], rb.at[parity, chunk(owner)], a_recv.at[1 + parity]).start()
 
-    def answer(i, carry):
-        t = lax.rem(gx * GY + gy + i, DEVICES)
-        tx, ty = lax.div(t, GY), lax.rem(t, GY)
+    def answer(dx, dy):
+        tx, ty = lax.rem(gx + dx, GX), lax.rem(gy + dy, GY)
         pltpu.make_async_remote_copy(
             src_ref=ob.at[chunk(ty * GX + tx)], dst_ref=rb.at[parity, chunk(owner)],
             send_sem=a_send.at[2], recv_sem=a_recv.at[1 + parity],
             device_id=(tx, ty), device_id_type=MESH,
         ).start()
+
+    def answers(dx, carry):
+        for dy in range(GY):
+            answer(dx, dy)
         return carry
 
-    lax.fori_loop(1, DEVICES, answer, 0)
+    for dy in range(1, GY):
+        answer(0, dy)
+    lax.fori_loop(1, GX, answers, 0)
 
     def backward(group):
         span(rb.at[group], OWNERS, 0, 1 + group).wait_recv()
         u = jnp.concatenate([rb[group, 0:128, :].T, rb[group, 128:256, :].T], axis=1)
         u = jnp.concatenate([u[0:SLOTS], u[SLOTS:]], axis=1)
         u_parts = halves(u)
-        inside = (p1_ref[group] + dot3((nt_h[...], nt_l[...]), u_parts)) * ie_ref[...]
+        inside = (p1_ref[group] + dot3(unpacked(narrow, 1280, 128, 64), u_parts)) * ie_ref[...]
         in_parts = halves(inside)
         both = (
             jnp.concatenate([in_parts[0], u_parts[0]], axis=0),
             jnp.concatenate([in_parts[1], u_parts[1]], axis=0),
         )
-        phi = dot3((fs_h[...], fs_l[...]), both)
+        phi = dot3(unpacked(mid, 1728, 128, 192), both)
         ext = jnp.concatenate([phi, u[16:32], u[40:48], jnp.zeros((8, NZ), f32)], axis=0)
         lhs[group] = dot3(halves(ext), (vh[...], vl[...]), nt=True)
         return dot3(halves(phi), (th[...], tl[...]), nt=True)
@@ -419,19 +466,17 @@
         return here - after, here - side
 
     tilted = backward(1)
-    for x in range(BX):
+
+    def gradient_row(x):
         fluid = fluid_at(x)
         c0, c1 = corrections(1, x)
         gp[0, x + 2] = fluid * (cot[0, x] - c0)
         gp[1, x + 2] = fluid * (cot[1, x] - c1)
         gp[2, x + 2] = fluid * (cot[2, x] - tilted[BY * x : BY * x + BY])
         sxp[x + 2] = adv[0, x]
-    nothing = jnp.zeros((2, BY, NZ), f32)
-    for c in range(3):
-        gp[c, 0:2] = nothing
-        gp[c, BX + 2 : BX + 4] = nothing
-    sxp[0:2] = nothing
-    sxp[BX + 2 : BX + 4] = nothing
+
+    for x in (0, 1, BX - 2, BX - 1):
+        gradient_row(x)
 
     k0, k1 = weights(adv[0, 0]), weights(adv[0, 1])
     k6, k7 = weights(adv[0, BX - 2]), weights(adv[0, BX - 1])
@@ -441,6 +486,16 @@
         cxs[0, c, 1] = k0[-1] * g0 + k1[-2] * g1
         cxs[1, c, 0] = k7[1] * g7 + k6[2] * g6
         cxs[1, c, 1] = k7[2] * g7
+    edges = [
+        remote(cxs.at[0], cxr.at[1], 4, left_x, gy),
+        remote(cxs.at[1], cxr.at[0], 5, right_x, gy),
+        remote(cys.at[0], cyr.at[1], 6, gx, left_y),
+        remote(cys.at[1], cyr.at[0], 7, gx, right_y),
+    ]
+    edges[0].start()
+    edges[1].start()
+    for x in range(2, BX - 2):
+        gradient_row(x)
     for x in range(BX):
         k = weights(adv[1, x])
         for c in range(3):
@@ -451,14 +506,14 @@
             one, two = k[1] * g, k[2] * g
             cys[1, c, 2 * x : 2 * x + 1, :] = one[BY - 1 : BY] + two[BY - 2 : BY - 1]
             cys[1, c, 2 * x + 1 : 2 * x + 2, :] = two[BY - 1 : BY]
-    edges = [
-        remote(cxs.at[0], cxr.at[1], 4, left_x, gy),
-        remote(cxs.at[1], cxr.at[0], 5, right_x, gy),
-        remote(cys.at[0], cyr.at[1], 6, gx, left_y),
-        remote(cys.at[1], cyr.at[0], 7, gx, right_y),
-    ]
-    for copy in edges:
-        copy.start()
+    edges[2].start()
+    edges[3].start()
+    nothing = jnp.zeros((2, BY, NZ), f32)
+    for c in range(3):
+        gp[c, 0:2] = nothing
+        gp[c, BX + 2 : BX + 4] = nothing
+    sxp[0:2] = nothing
+    sxp[BX + 2 : BX + 4] = nothing
 
     def adjoint_row(x, carry):
         kx = {}
@@ -506,19 +561,31 @@
             span(rbuf, OWNERS - 1, group, 0).wait_send()
 
 
+def section_factor(section_index):
+    section = lax.rem(section_index[0], 3)
+    step = lax.div(section_index[0], 3).astype(f32)
+    size = f32(0.2) + f32(0.2) * step / f32(63.0)
+    return size * jnp.where(section == 0, f32(1.0 / 3.0), jnp.where(section == 1, f32(0.5), f32(1.0)))
+
+
 def per_device(
     velocity_now, advecting, cotangent, building_height, section_index,
     vertical_modes, vertical_tilt, mode_rates,
 ):
-    constants = tables()
+    small = jnp.concatenate(
+        [
+            mode_rates.reshape(4, 128),
+            jnp.broadcast_to(section_factor(section_index), (4, 128)),
+            jnp.pad(building_height, ((0, 0), (0, 128 - BY))).astype(f32),
+        ]
+    )
     vmem = pl.BlockSpec(memory_space=pltpu.VMEM)
-    smem = pl.BlockSpec(memory_space=pltpu.SMEM)
-    hbm = pl.BlockSpec(memory_space=pl.ANY)
+    hbm = pl.BlockSpec(memory_space=pltpu.HBM)
     field = jax.ShapeDtypeStruct((3, BX, BY, NZ), f32)
     return pl.pallas_call(
         kernel,
         out_shape=(field, field),
-        in_specs=[hbm, hbm, hbm, vmem, smem, hbm, hbm, vmem, smem, hbm] + [vmem] * (len(constants) - 1),
+        in_specs=[hbm, hbm, hbm, vmem, hbm, hbm, hbm],
         out_specs=(vmem, vmem),
         scratch_shapes=[
             pltpu.VMEM((3, BX + 4, 32, NZ), f32),
@@ -526,7 +593,9 @@
             pltpu.VMEM((3, BX, BY, NZ), f32),
             pltpu.VMEM((NZ, NZ), f32),
             pltpu.VMEM((NZ, NZ), f32),
-            pltpu.VMEM((4, 512, 512), bf16),
+            pltpu.VMEM((LARGE, 512), bf16),
+            pltpu.VMEM((2 * MID, 256), bf16),
+            pltpu.VMEM((4 * NARROW, 128), bf16),
             pltpu.VMEM((3, BX, BY, NZ), f32),
             pltpu.VMEM((2, 160, NZ), f32),
             pltpu.VMEM((NZ, NZ), bf16),
@@ -551,15 +620,14 @@
             pltpu.SemaphoreType.DMA((3,)),
             pltpu.SemaphoreType.DMA((8,)),
             pltpu.SemaphoreType.DMA((8,)),
-            pltpu.SemaphoreType.DMA((6,)),
+            pltpu.SemaphoreType.DMA((12,)),
             pltpu.SemaphoreType.REGULAR,
         ],
         compiler_params=pltpu.CompilerParams(
-            collective_id=0, has_side_effects=True, vmem_limit_bytes=56 * 1024 * 1024
+            collective_id=0, has_side_effects=True, vmem_limit_bytes=52 * 1024 * 1024
         ),
     )(
-        velocity_now, advecting, cotangent, building_height, section_index,
-        vertical_modes, vertical_tilt, mode_rates.reshape(1, NZ), mode_rates, *constants,
+        velocity_now, advecting, cotangent, small, vertical_modes, vertical_tilt, tables(),
     )
 
 

time: 52.2 us -> 48.6 us (0.931)
  Pallas kernels: 47.7 us -> 43.8 us
  other arithmetic: 0 us -> 1.44 us
  local copies, waits for them, and re-layouts: 3.04 us -> 1.84 us
    pallas_call x1, Pallas kernels: 47.7 us -> 43.8 us  [per_device(): pl.pallas_call(kernel, out_shape=(field, field), in_specs=[hbm, hbm, hbm,...]
    unnamed x4 -> x2, local copies, waits for them, and re-layouts: 3.04 us -> 1.76 us
    concatenate x0 -> x1, other arithmetic: none -> 0.75 us  [per_device(): jnp.concatenate([mode_rates.reshape(4, 128), jnp.broadcast_to(section_fac...]
    convert_element_type x0 -> x1, other arithmetic: none -> 0.69 us  [per_device(): jnp.pad(building_height, ((0, 0), (0, 128 - BY))).astype(f32)]
where the time goes in v3:
time: 48.6 us; the launch traced here: 48.4 us
  Pallas kernels  43.8 us (90%)
  local copies, waits for them, and re-layouts  1.84 us (4%)
  other arithmetic  1.44 us (3%)
  between operations  1.32 us (3%)
    pallas_call x1, Pallas kernels, per_device(): pl.pallas_call(kernel, out_shape=(field, field), in_specs=[hbm, hbm, hbm,...  43.8 us
    unnamed x2, local copies, waits for them, and re-layouts  1.76 us

profile of v3, /device:TPU:1, one launch (start us, length us, event | category | flops | bytes accessed | tf_op | source)
XLA Modules:
  0.0 48.4 jit_solution(9368658609993552970)
XLA Ops:
  1.3 0.1 pad.6.clone
  1.4 0.7 %pad_convert_fusion = f32[8,128]{1,0:T(8,128)S(1)} fusion(s32[8,16]{1,0:T(8,128)} %param.12), kind=kLoop, calls=%fused_computation.1 | loop fusion | flops 1024 | bytes 4608 | tf_op jit(solution)/shard_map/convert_element_type | solution.py:579
  2.1 0.8 %pad_maximum_fusion.small = f32[16,128]{1,0:T(8,128)S(1)} fusion(f32[8,128]{1,0:T(8,128)S(1)} %pad_convert_fusion, f32[4,128]{1,0:T(4,128)} %bitcast.2, f32[16]{0:T(128)S(1)} %pad.6.clone), kind=kLoop, calls=%fused_computation | loop fusion | flops 4096 | bytes 14400 | tf_op jit(solution)/shard_map/concatenate | solution.py:575
  2.8 43.8 %shard_map.104 = (f32[3,8,16,512]{3,2,1,0:T(8,128)S(1)}, f32[3,8,16,512]{3,2,1,0:T(8,128)S(1)}) custom-call(f32[3,8,16,512]{3,2,1,0:T(8,128)} %vel_h.1, f32[3,8,16,512]{3,2,1,0:T(8,128)} %adv_h.1, f32[3,8,16,512]{3,2,1,0:T(8,128)} %cot_h.1, f32[16,128]{1,0:T(8,128)S(1)} %pad_maximum_fusion.small, f32[512,512]{1,0:T(8,128)} %vm_h.1, f32[512,512]{1,0:T(8,128)} %vt_h.1, ...), custom_call_target="tpu_custom_call" | custom-call | tf_op jit(solution)/shard_map/pallas_call | solution.py:585
  46.7 0.9 %copy.14 = f32[3,8,16,512]{3,2,1,0:T(8,128)} copy(f32[3,8,16,512]{3,2,1,0:T(8,128)S(1)} %get-tuple-element.4) | data formatting | bytes 1572864
  47.5 0.9 %copy.15 = f32[3,8,16,512]{3,2,1,0:T(8,128)} copy(f32[3,8,16,512]{3,2,1,0:T(8,128)S(1)} %get-tuple-element.5) | data formatting | bytes 1572864
  (1 shorter events, 0.0 us)

commit v4 on v3

--- a/solution.py
+++ b/solution.py
@@ -18,7 +18,7 @@
 OWNERS = DEVICES // 2
 OWNED = NZ // OWNERS // 2
 SLOTS = 64
-LARGE, MID, NARROW = 2304, 992, 688
+LARGE, MID, NARROW = 256, 992, 752
 f32, bf16 = jnp.float32, jnp.bfloat16
 
 
@@ -73,19 +73,16 @@
             for x in range(BX):
                 order[g, kind, x, x, kind, g] = 1.0
     order = order.reshape(256, 256)
-    rows = np.zeros((2, NX, OWNED, 2, 2, GX, OWNED))
-    cols = np.zeros((2, NX, OWNED, BX, 2, GX, OWNED))
+    rows = np.zeros((2, OWNED, NX, 2, 2, GX, OWNED))
     for group in range(2):
         for mode in range(OWNED):
             for g in range(GX):
                 for kind in range(2):
-                    rows[group, :, mode, kind, group, g, mode] = qx[8 * (g + kind) % NX]
-                for x in range(BX):
-                    cols[group, :, mode, x, group, g, mode] = qx[8 * g + x]
+                    rows[group, mode, :, kind, group, g, mode] = qx[8 * (g + kind) % NX]
     rows = rows.reshape(512, 128)
-    cols = cols.reshape(512, 512)
+    cols = qx.reshape(GX, BX, NX).transpose(2, 1, 0).reshape(NX, NX)
     wc = np.stack([qy[0::16], np.roll(qy[0::16], -1, axis=0)]).reshape(32, 256)
-    lam_x = np.broadcast_to(lx[None, :, None], (2, NX, OWNED)).reshape(512)
+    lam_x = np.tile(lx, 2 * OWNED)
 
     def columns(values):
         out = np.zeros((values.size, 128), ml_dtypes.bfloat16)
@@ -102,9 +99,9 @@
 
     exact = np.concatenate([order, order.T]).astype(ml_dtypes.bfloat16)
     lam_y = np.stack(split_const(ly, 3)).reshape(6, 128)
-    large = packed([cols, cols.T, rows.T], 512)
+    large = packed([rows.T], 512)
     mid = np.concatenate([exact, packed([qy, qy.T, wc, to_slots, from_slots], 256)])
-    narrow = np.concatenate([packed([sine, rows, near.T, wc.T], 128), columns(lam_x), columns(mu), lam_y])
+    narrow = np.concatenate([packed([sine, rows, near.T, wc.T, cols, cols.T], 128), columns(lam_x), columns(mu), lam_y])
     narrow = np.pad(narrow, ((0, 4 * NARROW - narrow.shape[0]), (0, 0)))
     mid = np.concatenate([mid[:MID], mid[MID:]], axis=1)
     narrow = np.concatenate([narrow[NARROW * i : NARROW * i + NARROW] for i in range(4)], axis=1)
@@ -131,27 +128,34 @@
     return lax.dot_general(a, b, dims, preferred_element_type=f32)
 
 
-def dot_narrow(a, b):
-    n = b[0].shape[1]
-    both = dot(a[0], jnp.concatenate([b[0], b[1]], axis=1))
-    return both[:, :n] + (both[:, n:] + dot(a[1], b[0]))
-
-
 def regroup(blocks):
     blocks = list(blocks)
-    group = lax.broadcasted_iota(jnp.int32, blocks[0].shape, 1) // 16
-    for step in (4, 2, 1):
+    lanes = 128 // len(blocks)
+    group = lax.broadcasted_iota(jnp.int32, blocks[0].shape, 1) // lanes
+    step = len(blocks) // 2
+    while step:
         low = (group & step) == 0
-        for i in range(8):
+        for i in range(len(blocks)):
             if not i & step:
                 a, b = blocks[i], blocks[i + step]
-                blocks[i] = jnp.where(low, a, pltpu.roll(b, 16 * step, 1))
-                blocks[i + step] = jnp.where(low, pltpu.roll(a, 128 - 16 * step, 1), b)
+                blocks[i] = jnp.where(low, a, pltpu.roll(b, lanes * step, 1))
+                blocks[i + step] = jnp.where(low, pltpu.roll(a, 128 - lanes * step, 1), b)
+        step //= 2
     return blocks
 
 
+def regroup_wide(blocks):
+    out = []
+    for right in range(2):
+        quads = [regroup([b[:, 128 * right : 128 * right + 128] for b in blocks[4 * n : 4 * n + 4]]) for n in range(2)]
+        out.extend(jnp.concatenate([a, b], axis=1) for a, b in zip(*quads))
+    return out
+
+
 def dot3(a, b, nt=False):
-    return dot(a[0], b[0], nt) + (dot(a[0], b[1], nt) + dot(a[1], b[0], nt))
+    n = a[0].shape[0]
+    both = dot(jnp.concatenate([a[0], a[1]], axis=0), b[0], nt)
+    return both[:n] + (dot(a[0], b[1], nt) + both[n:])
 
 
 def wide(column, lanes):
@@ -185,7 +189,7 @@
     next_ref, adj_ref,
     vb, adv, cot, vm_ref, vt_ref, large, mid, narrow,
     sv, lhs, vh, vl, th, tl, ys, yr, sb, rbuf, ob, rb, gp, sxp, cxs, cxr, cys, cyr,
-    p1_ref, ie_ref,
+    p1_ref, ie_ref, cs,
     a_send, a_recv, h_send, h_recv, l_sem, all_sem,
 ):
     gx, gy = lax.axis_index("gx"), lax.axis_index("gy")
@@ -261,7 +265,7 @@
     for n in range(6, 10):
         loads[n].wait()
     rate_row = jnp.concatenate([small[n : n + 1, :] for n in range(4)], axis=1)
-    ie_ref[...] = 1.0 / (summed(narrow[2560:2688, :]) + rate_row)
+    ie_ref[...] = 1.0 / (summed(narrow[2816:2944, :]) + rate_row)
 
     factor = small[4:5, 0:1]
     scale = factor * f32(-1.0 / 12.0)
@@ -392,15 +396,23 @@
     along = dot3(halves(jnp.concatenate([rows[0], rows[4], rows[1], rows[5]], axis=0)), unpacked(mid, 512, 256, 256))
     columns = halves(jnp.concatenate([rows[2], rows[6]], axis=0))
     columns = dot(columns[0], mid[0:256, :]) + dot(columns[1], mid[0:256, :])
-    columns = jnp.concatenate([columns[:, 32 * x : 32 * x + 32] for x in range(BX)], axis=0)
-    inner = halves(dot_narrow(unpacked(large, 0, 512, 512), halves(columns)))
+    for n in range(2):
+        cs[n] = columns[:, 128 * n : 128 * n + 128]
+    picked = [
+        jnp.concatenate([cs[n, pl.ds(32 * half + m, GX, stride=OWNED), :] for n in range(2)], axis=1)
+        for half in range(2)
+        for m in range(OWNED)
+    ]
+    columns = halves(jnp.concatenate(regroup_wide(picked), axis=0))
+    inner = dot3(unpacked(narrow, 2048, 64, 64), columns)
+    inner = halves(jnp.concatenate([inner[:, 32 * n : 32 * n + 32] for n in range(8)], axis=0))
     along = halves(along)
     row_table, edge_table = unpacked(narrow, 256, 512, 128), unpacked(mid, 1536, 32, 256)
     left = [jnp.concatenate([row_table[i], inner[i]], axis=1) for i in range(2)]
     right = [jnp.concatenate([along[i], edge_table[i]], axis=0) for i in range(2)]
     hat = dot3(left, right)
     row = lax.broadcasted_iota(jnp.int32, (512, 128), 0)
-    row_mode = lax.rem(row, OWNED) + OWNED * lax.div(row, 256)
+    row_mode = lax.div(row, NX)
     rate = jnp.zeros((512, 128), f32)
     lane = lax.broadcasted_iota(jnp.int32, (1, 128), 1)
     first_lane = lax.rem(owner, 128 // OWNED) * OWNED
@@ -409,13 +421,21 @@
         for m in range(OWNED):
             one = jnp.sum(jnp.where(lane == first_lane + m, rates, 0.0), axis=1, keepdims=True)
             rate = jnp.where(row_mode == OWNED * half + m, one, rate)
-    lam_y = narrow[2688:2704, :].astype(f32)
+    lam_y = narrow[2944:2960, :].astype(f32)
     lam_y = [lam_y[n : n + 1] + (lam_y[n + 2 : n + 3] + lam_y[n + 4 : n + 5]) for n in range(2)]
     lam_y = jnp.concatenate(lam_y, axis=1)
-    hat = halves(hat / (wide(rate + summed(narrow[2048:2560, :]), 256) + lam_y))
-    along = dot3(halves(dot3(unpacked(large, 2048, 128, 512), hat)), unpacked(mid, 1024, 256, 256))
-    columns = dot_narrow(unpacked(large, 1024, 512, 512), halves(dot3(hat, unpacked(narrow, 1536, 256, 32))))
-    columns = halves(jnp.concatenate([columns[64 * x : 64 * x + 64, :] for x in range(BX)], axis=1))
+    hat = halves(hat / (wide(rate + summed(narrow[2304:2816, :]), 256) + lam_y))
+    along = dot3(halves(dot3(unpacked(large, 0, 128, 512), hat)), unpacked(mid, 1024, 256, 256))
+    inner = dot3(hat, unpacked(narrow, 1536, 256, 32))
+    inner = halves(jnp.concatenate([inner[NX * n : NX * n + NX] for n in range(8)], axis=1))
+    columns = dot3(unpacked(narrow, 2176, 64, 64), inner)
+    picked = regroup_wide([columns[8 * x : 8 * x + 8] for x in range(BX)])
+    for half in range(2):
+        for m in range(OWNED):
+            for n in range(2):
+                block = picked[OWNED * half + m][:, 128 * n : 128 * n + 128]
+                cs[n, pl.ds(32 * half + m, GX, stride=OWNED), :] = block
+    columns = halves(jnp.concatenate([cs[0], cs[1]], axis=1))
     columns = dot(columns[0], mid[256:512, :]) + dot(columns[1], mid[256:512, :])
     nothing = jnp.zeros((32, 256), f32)
     rows = [along[0:32], along[64:96], columns[0:32], nothing, along[32:64], along[96:128], columns[32:64], nothing]
@@ -561,6 +581,17 @@
             span(rbuf, OWNERS - 1, group, 0).wait_send()
 
 
+def write_out(next_ref, adj_ref, next_out, adj_out, sems):
+    copies = [
+        pltpu.make_async_copy(next_ref, next_out, sems.at[0]),
+        pltpu.make_async_copy(adj_ref, adj_out, sems.at[1]),
+    ]
+    for copy in copies:
+        copy.start()
+    for copy in copies:
+        copy.wait()
+
+
 def section_factor(section_index):
     section = lax.rem(section_index[0], 3)
     step = lax.div(section_index[0], 3).astype(f32)
@@ -582,7 +613,7 @@
     vmem = pl.BlockSpec(memory_space=pltpu.VMEM)
     hbm = pl.BlockSpec(memory_space=pltpu.HBM)
     field = jax.ShapeDtypeStruct((3, BX, BY, NZ), f32)
-    return pl.pallas_call(
+    results = pl.pallas_call(
         kernel,
         out_shape=(field, field),
         in_specs=[hbm, hbm, hbm, vmem, hbm, hbm, hbm],
@@ -616,6 +647,7 @@
             pltpu.VMEM((2, 3, 16, NZ), f32),
             pltpu.VMEM((2, 128, NZ), f32),
             pltpu.VMEM((128, NZ), f32),
+            pltpu.VMEM((2, 64, 128), f32),
             pltpu.SemaphoreType.DMA((3,)),
             pltpu.SemaphoreType.DMA((3,)),
             pltpu.SemaphoreType.DMA((8,)),
@@ -629,6 +661,14 @@
     )(
         velocity_now, advecting, cotangent, small, vertical_modes, vertical_tilt, tables(),
     )
+    return pl.pallas_call(
+        write_out,
+        out_shape=(field, field),
+        in_specs=[vmem, vmem],
+        out_specs=(hbm, hbm),
+        scratch_shapes=[pltpu.SemaphoreType.DMA((2,))],
+        compiler_params=pltpu.CompilerParams(vmem_limit_bytes=8 * 1024 * 1024),
+    )(*results)
 
 
 def solution(mesh):

time: 48.6 us -> 46.9 us (0.965)
  local copies, waits for them, and re-layouts: 1.84 us -> 0.08 us
    unnamed x2 -> x0, local copies, waits for them, and re-layouts: 1.76 us -> none
    pallas_call x0 -> x1, Pallas kernels: none -> 1.16 us  [per_device(): pl.pallas_call(write_out, out_shape=(field, field), in_specs=[vmem, vmem]...]
    pallas_call x1, Pallas kernels: 43.8 us -> 42.7 us  [per_device(): pl.pallas_call(kernel, out_shape=(field, field), in_specs=[hbm, hbm, hbm,...]
where the time goes in v4:
time: 46.9 us; the launch traced here: 46.7 us
  Pallas kernels  43.9 us (94%)
  other arithmetic  1.44 us (3%)
  between operations  1.32 us (3%)
    pallas_call x1, Pallas kernels, per_device(): pl.pallas_call(kernel, out_shape=(field, field), in_specs=[hbm, hbm, hbm,...  42.7 us
    pallas_call x1, Pallas kernels, per_device(): pl.pallas_call(write_out, out_shape=(field, field), in_specs=[vmem, vmem]...  1.16 us

profile of v4, /device:TPU:1, one launch (start us, length us, event | category | flops | bytes accessed | tf_op | source)
XLA Modules:
  0.0 46.7 jit_solution(7760887818818312618)
XLA Ops:
  1.3 0.1 pad.6.clone
  1.4 0.7 %pad_convert_fusion = f32[8,128]{1,0:T(8,128)S(1)} fusion(s32[8,16]{1,0:T(8,128)} %param.12), kind=kLoop, calls=%fused_computation.1 | loop fusion | flops 1024 | bytes 4608 | tf_op jit(solution)/shard_map/convert_element_type | solution.py:610
  2.1 0.8 %pad_maximum_fusion.small = f32[16,128]{1,0:T(8,128)S(1)} fusion(f32[8,128]{1,0:T(8,128)S(1)} %pad_convert_fusion, f32[4,128]{1,0:T(4,128)} %bitcast.2, f32[16]{0:T(128)S(1)} %pad.6.clone), kind=kLoop, calls=%fused_computation | loop fusion | flops 4096 | bytes 14400 | tf_op jit(solution)/shard_map/concatenate | solution.py:606
  2.8 42.7 %shard_map.104 = (f32[3,8,16,512]{3,2,1,0:T(8,128)S(1)}, f32[3,8,16,512]{3,2,1,0:T(8,128)S(1)}) custom-call(f32[3,8,16,512]{3,2,1,0:T(8,128)} %vel_h.1, f32[3,8,16,512]{3,2,1,0:T(8,128)} %adv_h.1, f32[3,8,16,512]{3,2,1,0:T(8,128)} %cot_h.1, f32[16,128]{1,0:T(8,128)S(1)} %pad_maximum_fusion.small, f32[512,512]{1,0:T(8,128)} %vm_h.1, f32[512,512]{1,0:T(8,128)} %vt_h.1, ...), custom_call_target="tpu_custom_call" | custom-call | tf_op jit(solution)/shard_map/pallas_call | solution.py:616
  45.5 1.2 %shard_map.105 = (f32[3,8,16,512]{3,2,1,0:T(8,128)}, f32[3,8,16,512]{3,2,1,0:T(8,128)}) custom-call(f32[3,8,16,512]{3,2,1,0:T(8,128)S(1)} %get-tuple-element.4.next_ref, f32[3,8,16,512]{3,2,1,0:T(8,128)S(1)} %get-tuple-element.5.adj_ref), custom_call_target="tpu_custom_call" | custom-call | tf_op jit(solution)/shard_map/pallas_call | solution.py:664
  (1 shorter events, 0.0 us)

commit v5 on v4

--- a/solution.py
+++ b/solution.py
@@ -228,13 +228,6 @@
     ]
     for n in (0, 3, 1, 2, 6, 7, 8, 9, 10, 11, 4, 5):
         loads[n].start()
-    loads[0].wait()
-
-    for c in range(3):
-        for x in range(BX):
-            ys[0, c, 2 * x : 2 * x + 2, :] = vb[c, x + 2, 8:10, :]
-            ys[1, c, 2 * x : 2 * x + 2, :] = vb[c, x + 2, 6 + BY : 8 + BY, :]
-
     pl.semaphore_wait(barrier, GX + GY - 2)
 
     def remote(src, dst, n, x, y):
@@ -249,11 +242,18 @@
         remote(ys.at[0], yr.at[1], 2, gx, left_y),
         remote(ys.at[1], yr.at[0], 3, gx, right_y),
     ]
-    for n in (2, 3, 0, 1):
-        halo[n].start()
 
     for i in range(1, GY):
         pl.semaphore_signal(all_sem, inc=1, device_id=(gx, lax.rem(gy + i, GY)), device_id_type=MESH)
+
+    loads[0].wait()
+
+    for c in range(3):
+        for x in range(BX):
+            ys[0, c, 2 * x : 2 * x + 2, :] = vb[c, x + 2, 8:10, :]
+            ys[1, c, 2 * x : 2 * x + 2, :] = vb[c, x + 2, 6 + BY : 8 + BY, :]
+    halo[2].start()
+    halo[3].start()
 
     loads[1].wait()
     loads[2].wait()
@@ -355,8 +355,87 @@
     forward(1, cot)
     pl.semaphore_wait(all_sem, GY - 1)
     to_owners(1)
+    halo[0].start()
+    halo[1].start()
 
     loads[4].wait()
+    def own():
+        loads[5].wait()
+        span(rbuf, DEVICES, 0, 0).wait_recv()
+        sides = [
+            regroup([rbuf[32 * (8 * half + i) : 32 * (8 * half + i) + 32, :] for i in range(8)])
+            for half in range(2)
+        ]
+        rows = [jnp.concatenate([sides[0][j], sides[1][j]], axis=1) for j in range(8)]
+        along = dot3(halves(jnp.concatenate([rows[0], rows[4], rows[1], rows[5]], axis=0)), unpacked(mid, 512, 256, 256))
+        columns = halves(jnp.concatenate([rows[2], rows[6]], axis=0))
+        columns = dot(columns[0], mid[0:256, :]) + dot(columns[1], mid[0:256, :])
+        for n in range(2):
+            cs[n] = columns[:, 128 * n : 128 * n + 128]
+        picked = [
+            jnp.concatenate([cs[n, pl.ds(32 * half + m, GX, stride=OWNED), :] for n in range(2)], axis=1)
+            for half in range(2)
+            for m in range(OWNED)
+        ]
+        columns = halves(jnp.concatenate(regroup_wide(picked), axis=0))
+        inner = dot3(unpacked(narrow, 2048, 64, 64), columns)
+        inner = halves(jnp.concatenate([inner[:, 32 * n : 32 * n + 32] for n in range(8)], axis=0))
+        along = halves(along)
+        row_table, edge_table = unpacked(narrow, 256, 512, 128), unpacked(mid, 1536, 32, 256)
+        left = [jnp.concatenate([row_table[i], inner[i]], axis=1) for i in range(2)]
+        right = [jnp.concatenate([along[i], edge_table[i]], axis=0) for i in range(2)]
+        hat = dot3(left, right)
+        row = lax.broadcasted_iota(jnp.int32, (512, 128), 0)
+        row_mode = lax.div(row, NX)
+        rate = jnp.zeros((512, 128), f32)
+        lane = lax.broadcasted_iota(jnp.int32, (1, 128), 1)
+        first_lane = lax.rem(owner, 128 // OWNED) * OWNED
+        for half in range(2):
+            rates = small[pl.ds(2 * half + lax.div(owner, 128 // OWNED), 1), :]
+            for m in range(OWNED):
+                one = jnp.sum(jnp.where(lane == first_lane + m, rates, 0.0), axis=1, keepdims=True)
+                rate = jnp.where(row_mode == OWNED * half + m, one, rate)
+        lam_y = narrow[2944:2960, :].astype(f32)
+        lam_y = [lam_y[n : n + 1] + (lam_y[n + 2 : n + 3] + lam_y[n + 4 : n + 5]) for n in range(2)]
+        lam_y = jnp.concatenate(lam_y, axis=1)
+        hat = halves(hat / (wide(rate + summed(narrow[2304:2816, :]), 256) + lam_y))
+        along = dot3(halves(dot3(unpacked(large, 0, 128, 512), hat)), unpacked(mid, 1024, 256, 256))
+        inner = dot3(hat, unpacked(narrow, 1536, 256, 32))
+        inner = halves(jnp.concatenate([inner[NX * n : NX * n + NX] for n in range(8)], axis=1))
+        columns = dot3(unpacked(narrow, 2176, 64, 64), inner)
+        picked = regroup_wide([columns[8 * x : 8 * x + 8] for x in range(BX)])
+        for half in range(2):
+            for m in range(OWNED):
+                for n in range(2):
+                    block = picked[OWNED * half + m][:, 128 * n : 128 * n + 128]
+                    cs[n, pl.ds(32 * half + m, GX, stride=OWNED), :] = block
+        columns = halves(jnp.concatenate([cs[0], cs[1]], axis=1))
+        columns = dot(columns[0], mid[256:512, :]) + dot(columns[1], mid[256:512, :])
+        nothing = jnp.zeros((32, 256), f32)
+        rows = [along[0:32], along[64:96], columns[0:32], nothing, along[32:64], along[96:128], columns[32:64], nothing]
+        for half in range(2):
+            for i, block in enumerate(regroup([r[:, 128 * half : 128 * half + 128] for r in rows])):
+                ob[32 * (8 * half + i) : 32 * (8 * half + i) + 32, :] = block
+
+        pltpu.make_async_copy(ob.at[chunk(place)], rb.at[parity, chunk(owner)], a_recv.at[1 + parity]).start()
+
+        def answer(dx, dy):
+            tx, ty = lax.rem(gx + dx, GX), lax.rem(gy + dy, GY)
+            pltpu.make_async_remote_copy(
+                src_ref=ob.at[chunk(ty * GX + tx)], dst_ref=rb.at[parity, chunk(owner)],
+                send_sem=a_send.at[2], recv_sem=a_recv.at[1 + parity],
+                device_id=(tx, ty), device_id_type=MESH,
+            ).start()
+
+        def answers(dx, carry):
+            for dy in range(GY):
+                answer(dx, dy)
+            return carry
+
+        for dy in range(1, GY):
+            answer(0, dy)
+        lax.fori_loop(1, GX, answers, 0)
+
     halo[2].wait()
     halo[3].wait()
     for c in range(3):
@@ -378,6 +457,7 @@
         return carry
 
     lax.fori_loop(2, BX - 2, section_row, 0)
+    pl.when(parity == 1)(own)
     halo[0].wait()
     halo[1].wait()
     lax.fori_loop(0, 2, section_row, 0)
@@ -385,82 +465,6 @@
     forward(0, sv)
 
     to_owners(0)
-
-    loads[5].wait()
-    span(rbuf, DEVICES, 0, 0).wait_recv()
-    sides = [
-        regroup([rbuf[32 * (8 * half + i) : 32 * (8 * half + i) + 32, :] for i in range(8)])
-        for half in range(2)
-    ]
-    rows = [jnp.concatenate([sides[0][j], sides[1][j]], axis=1) for j in range(8)]
-    along = dot3(halves(jnp.concatenate([rows[0], rows[4], rows[1], rows[5]], axis=0)), unpacked(mid, 512, 256, 256))
-    columns = halves(jnp.concatenate([rows[2], rows[6]], axis=0))
-    columns = dot(columns[0], mid[0:256, :]) + dot(columns[1], mid[0:256, :])
-    for n in range(2):
-        cs[n] = columns[:, 128 * n : 128 * n + 128]
-    picked = [
-        jnp.concatenate([cs[n, pl.ds(32 * half + m, GX, stride=OWNED), :] for n in range(2)], axis=1)
-        for half in range(2)
-        for m in range(OWNED)
-    ]
-    columns = halves(jnp.concatenate(regroup_wide(picked), axis=0))
-    inner = dot3(unpacked(narrow, 2048, 64, 64), columns)
-    inner = halves(jnp.concatenate([inner[:, 32 * n : 32 * n + 32] for n in range(8)], axis=0))
-    along = halves(along)
-    row_table, edge_table = unpacked(narrow, 256, 512, 128), unpacked(mid, 1536, 32, 256)
-    left = [jnp.concatenate([row_table[i], inner[i]], axis=1) for i in range(2)]
-    right = [jnp.concatenate([along[i], edge_table[i]], axis=0) for i in range(2)]
-    hat = dot3(left, right)
-    row = lax.broadcasted_iota(jnp.int32, (512, 128), 0)
-    row_mode = lax.div(row, NX)
-    rate = jnp.zeros((512, 128), f32)
-    lane = lax.broadcasted_iota(jnp.int32, (1, 128), 1)
-    first_lane = lax.rem(owner, 128 // OWNED) * OWNED
-    for half in range(2):
-        rates = small[pl.ds(2 * half + lax.div(owner, 128 // OWNED), 1), :]
-        for m in range(OWNED):
-            one = jnp.sum(jnp.where(lane == first_lane + m, rates, 0.0), axis=1, keepdims=True)
-            rate = jnp.where(row_mode == OWNED * half + m, one, rate)
-    lam_y = narrow[2944:2960, :].astype(f32)
-    lam_y = [lam_y[n : n + 1] + (lam_y[n + 2 : n + 3] + lam_y[n + 4 : n + 5]) for n in range(2)]
-    lam_y = jnp.concatenate(lam_y, axis=1)
-    hat = halves(hat / (wide(rate + summed(narrow[2304:2816, :]), 256) + lam_y))
-    along = dot3(halves(dot3(unpacked(large, 0, 128, 512), hat)), unpacked(mid, 1024, 256, 256))
-    inner = dot3(hat, unpacked(narrow, 1536, 256, 32))
-    inner = halves(jnp.concatenate([inner[NX * n : NX * n + NX] for n in range(8)], axis=1))
-    columns = dot3(unpacked(narrow, 2176, 64, 64), inner)
-    picked = regroup_wide([columns[8 * x : 8 * x + 8] for x in range(BX)])
-    for half in range(2):
-        for m in range(OWNED):
-            for n in range(2):
-                block = picked[OWNED * half + m][:, 128 * n : 128 * n + 128]
-                cs[n, pl.ds(32 * half + m, GX, stride=OWNED), :] = block
-    columns = halves(jnp.concatenate([cs[0], cs[1]], axis=1))
-    columns = dot(columns[0], mid[256:512, :]) + dot(columns[1], mid[256:512, :])
-    nothing = jnp.zeros((32, 256), f32)
-    rows = [along[0:32], along[64:96], columns[0:32], nothing, along[32:64], along[96:128], columns[32:64], nothing]
-    for half in range(2):
-        for i, block in enumerate(regroup([r[:, 128 * half : 128 * half + 128] for r in rows])):
-            ob[32 * (8 * half + i) : 32 * (8 * half + i) + 32, :] = block
-
-    pltpu.make_async_copy(ob.at[chunk(place)], rb.at[parity, chunk(owner)], a_recv.at[1 + parity]).start()
-
-    def answer(dx, dy):
-        tx, ty = lax.rem(gx + dx, GX), lax.rem(gy + dy, GY)
-        pltpu.make_async_remote_copy(
-            src_ref=ob.at[chunk(ty * GX + tx)], dst_ref=rb.at[parity, chunk(owner)],
-            send_sem=a_send.at[2], recv_sem=a_recv.at[1 + parity],
-            device_id=(tx, ty), device_id_type=MESH,
-        ).start()
-
-    def answers(dx, carry):
-        for dy in range(GY):
-            answer(dx, dy)
-        return carry
-
-    for dy in range(1, GY):
-        answer(0, dy)
-    lax.fori_loop(1, GX, answers, 0)
 
     def backward(group):
         span(rb.at[group], OWNERS, 0, 1 + group).wait_recv()
@@ -476,7 +480,10 @@
         phi = dot3(unpacked(mid, 1728, 128, 192), both)
         ext = jnp.concatenate([phi, u[16:32], u[40:48], jnp.zeros((8, NZ), f32)], axis=0)
         lhs[group] = dot3(halves(ext), (vh[...], vl[...]), nt=True)
-        return dot3(halves(phi), (th[...], tl[...]), nt=True)
+        return halves(phi)
+
+    def tilt(phi):
+        return dot3(phi, (th[...], tl[...]), nt=True)
 
     def corrections(group, x):
         here = lhs[group, BY * x : BY * x + BY, :]
@@ -485,37 +492,52 @@
         side = jnp.where(last, lhs[group, 144 + x : 145 + x, :], jnp.roll(here, -1, 0))
         return here - after, here - side
 
-    tilted = backward(1)
+    phi = backward(1)
 
     def gradient_row(x):
         fluid = fluid_at(x)
         c0, c1 = corrections(1, x)
         gp[0, x + 2] = fluid * (cot[0, x] - c0)
         gp[1, x + 2] = fluid * (cot[1, x] - c1)
-        gp[2, x + 2] = fluid * (cot[2, x] - tilted[BY * x : BY * x + BY])
         sxp[x + 2] = adv[0, x]
+
+    def gradient_row_z(x):
+        gp[2, x + 2] = fluid_at(x) * (cot[2, x] - tilted[BY * x : BY * x + BY])
 
     for x in (0, 1, BX - 2, BX - 1):
         gradient_row(x)
 
     k0, k1 = weights(adv[0, 0]), weights(adv[0, 1])
     k6, k7 = weights(adv[0, BX - 2]), weights(adv[0, BX - 1])
-    for c in range(3):
+    edges = [
+        remote(cxs.at[0, pl.ds(0, 2)], cxr.at[1, pl.ds(0, 2)], 4, left_x, gy),
+        remote(cxs.at[1, pl.ds(0, 2)], cxr.at[0, pl.ds(0, 2)], 5, right_x, gy),
+        remote(cys.at[0], cyr.at[1], 6, gx, left_y),
+        remote(cys.at[1], cyr.at[0], 7, gx, right_y),
+        remote(cxs.at[0, pl.ds(2, 1)], cxr.at[1, pl.ds(2, 1)], 8, left_x, gy),
+        remote(cxs.at[1, pl.ds(2, 1)], cxr.at[0, pl.ds(2, 1)], 9, right_x, gy),
+    ]
+
+    def contributions_x(c):
         g0, g1, g6, g7 = gp[c, 2], gp[c, 3], gp[c, BX], gp[c, BX + 1]
         cxs[0, c, 0] = k0[-2] * g0
         cxs[0, c, 1] = k0[-1] * g0 + k1[-2] * g1
         cxs[1, c, 0] = k7[1] * g7 + k6[2] * g6
         cxs[1, c, 1] = k7[2] * g7
-    edges = [
-        remote(cxs.at[0], cxr.at[1], 4, left_x, gy),
-        remote(cxs.at[1], cxr.at[0], 5, right_x, gy),
-        remote(cys.at[0], cyr.at[1], 6, gx, left_y),
-        remote(cys.at[1], cyr.at[0], 7, gx, right_y),
-    ]
+
+    contributions_x(0)
+    contributions_x(1)
     edges[0].start()
     edges[1].start()
+    tilted = tilt(phi)
+    for x in (0, 1, BX - 2, BX - 1):
+        gradient_row_z(x)
+    contributions_x(2)
+    edges[4].start()
+    edges[5].start()
     for x in range(2, BX - 2):
         gradient_row(x)
+        gradient_row_z(x)
     for x in range(BX):
         k = weights(adv[1, x])
         for c in range(3):
@@ -528,6 +550,7 @@
             cys[1, c, 2 * x + 1 : 2 * x + 2, :] = two[BY - 1 : BY]
     edges[2].start()
     edges[3].start()
+    pl.when(parity == 0)(own)
     nothing = jnp.zeros((2, BY, NZ), f32)
     for c in range(3):
         gp[c, 0:2] = nothing
@@ -552,7 +575,7 @@
 
     lax.fori_loop(0, BX, adjoint_row, 0)
 
-    tilted = backward(0)
+    tilted = tilt(backward(0))
     for x in range(BX):
         c0, c1 = corrections(0, x)
         next_ref[0, x] = sv[0, x] - c0
@@ -650,8 +673,8 @@
             pltpu.VMEM((2, 64, 128), f32),
             pltpu.SemaphoreType.DMA((3,)),
             pltpu.SemaphoreType.DMA((3,)),
-            pltpu.SemaphoreType.DMA((8,)),
-            pltpu.SemaphoreType.DMA((8,)),
+            pltpu.SemaphoreType.DMA((10,)),
+            pltpu.SemaphoreType.DMA((10,)),
             pltpu.SemaphoreType.DMA((12,)),
             pltpu.SemaphoreType.REGULAR,
         ],

time: 46.9 us -> 44.7 us (0.953)
  Pallas kernels: 43.9 us -> 41.7 us
    pallas_call x1, Pallas kernels: 42.7 us -> 40.6 us  [per_device(): pl.pallas_call(kernel, out_shape=(field, field), in_specs=[hbm, hbm, hbm,...]
where the time goes in v5:
time: 44.7 us; the launch traced here: 44.6 us
  Pallas kernels  41.7 us (93%)
  other arithmetic  1.44 us (3%)
  between operations  1.32 us (3%)
    pallas_call x1, Pallas kernels, per_device(): pl.pallas_call(kernel, out_shape=(field, field), in_specs=[hbm, hbm, hbm,...  40.6 us
    pallas_call x1, Pallas kernels, per_device(): pl.pallas_call(write_out, out_shape=(field, field), in_specs=[vmem, vmem]...  1.16 us

profile of v5, /device:TPU:1, one launch (start us, length us, event | category | flops | bytes accessed | tf_op | source)
XLA Modules:
  0.0 44.6 jit_solution(4346688976988420589)
XLA Ops:
  1.3 0.1 pad.6.clone
  1.4 0.7 %pad_convert_fusion = f32[8,128]{1,0:T(8,128)S(1)} fusion(s32[8,16]{1,0:T(8,128)} %param.12), kind=kLoop, calls=%fused_computation.1 | loop fusion | flops 1024 | bytes 4608 | tf_op jit(solution)/shard_map/convert_element_type | solution.py:633
  2.1 0.8 %pad_maximum_fusion.small = f32[16,128]{1,0:T(8,128)S(1)} fusion(f32[8,128]{1,0:T(8,128)S(1)} %pad_convert_fusion, f32[4,128]{1,0:T(4,128)} %bitcast.2, f32[16]{0:T(128)S(1)} %pad.6.clone), kind=kLoop, calls=%fused_computation | loop fusion | flops 4096 | bytes 14400 | tf_op jit(solution)/shard_map/concatenate | solution.py:629
  2.8 40.6 %shard_map.104 = (f32[3,8,16,512]{3,2,1,0:T(8,128)S(1)}, f32[3,8,16,512]{3,2,1,0:T(8,128)S(1)}) custom-call(f32[3,8,16,512]{3,2,1,0:T(8,128)} %vel_h.1, f32[3,8,16,512]{3,2,1,0:T(8,128)} %adv_h.1, f32[3,8,16,512]{3,2,1,0:T(8,128)} %cot_h.1, f32[16,128]{1,0:T(8,128)S(1)} %pad_maximum_fusion.small, f32[512,512]{1,0:T(8,128)} %vm_h.1, f32[512,512]{1,0:T(8,128)} %vt_h.1, ...), custom_call_target="tpu_custom_call" | custom-call | tf_op jit(solution)/shard_map/pallas_call | solution.py:639
  43.4 1.2 %shard_map.105 = (f32[3,8,16,512]{3,2,1,0:T(8,128)}, f32[3,8,16,512]{3,2,1,0:T(8,128)}) custom-call(f32[3,8,16,512]{3,2,1,0:T(8,128)S(1)} %get-tuple-element.4.next_ref, f32[3,8,16,512]{3,2,1,0:T(8,128)S(1)} %get-tuple-element.5.adj_ref), custom_call_target="tpu_custom_call" | custom-call | tf_op jit(solution)/shard_map/pallas_call | solution.py:687
  (1 shorter events, 0.0 us)

commit v6 on v5

--- a/solution.py
+++ b/solution.py
@@ -436,6 +436,7 @@
             answer(0, dy)
         lax.fori_loop(1, GX, answers, 0)
 
+    pl.when(parity == 1)(own)
     halo[2].wait()
     halo[3].wait()
     for c in range(3):
@@ -457,7 +458,6 @@
         return carry
 
     lax.fori_loop(2, BX - 2, section_row, 0)
-    pl.when(parity == 1)(own)
     halo[0].wait()
     halo[1].wait()
     lax.fori_loop(0, 2, section_row, 0)

time: 44.7 us -> 45.6 us (1.020)
  Pallas kernels: 41.7 us -> 42.6 us
    pallas_call x1, Pallas kernels: 40.6 us -> 41.4 us  [per_device(): pl.pallas_call(kernel, out_shape=(field, field), in_specs=[hbm, hbm, hbm,...]
where the time goes in v6:
time: 45.6 us; the launch traced here: 45.4 us
  Pallas kernels  42.6 us (93%)
  other arithmetic  1.44 us (3%)
  between operations  1.32 us (3%)
    pallas_call x1, Pallas kernels, per_device(): pl.pallas_call(kernel, out_shape=(field, field), in_specs=[hbm, hbm, hbm,...  41.4 us
    pallas_call x1, Pallas kernels, per_device(): pl.pallas_call(write_out, out_shape=(field, field), in_specs=[vmem, vmem]...  1.16 us

profile of v6, /device:TPU:1, one launch (start us, length us, event | category | flops | bytes accessed | tf_op | source)
XLA Modules:
  0.0 45.4 jit_solution(5658731936696977006)
XLA Ops:
  1.3 0.1 pad.6.clone
  1.4 0.7 %pad_convert_fusion = f32[8,128]{1,0:T(8,128)S(1)} fusion(s32[8,16]{1,0:T(8,128)} %param.12), kind=kLoop, calls=%fused_computation.1 | loop fusion | flops 1024 | bytes 4608 | tf_op jit(solution)/shard_map/convert_element_type | solution.py:633
  2.1 0.8 %pad_maximum_fusion.small = f32[16,128]{1,0:T(8,128)S(1)} fusion(f32[8,128]{1,0:T(8,128)S(1)} %pad_convert_fusion, f32[4,128]{1,0:T(4,128)} %bitcast.2, f32[16]{0:T(128)S(1)} %pad.6.clone), kind=kLoop, calls=%fused_computation | loop fusion | flops 4096 | bytes 14400 | tf_op jit(solution)/shard_map/concatenate | solution.py:629
  2.8 41.4 %shard_map.104 = (f32[3,8,16,512]{3,2,1,0:T(8,128)S(1)}, f32[3,8,16,512]{3,2,1,0:T(8,128)S(1)}) custom-call(f32[3,8,16,512]{3,2,1,0:T(8,128)} %vel_h.1, f32[3,8,16,512]{3,2,1,0:T(8,128)} %adv_h.1, f32[3,8,16,512]{3,2,1,0:T(8,128)} %cot_h.1, f32[16,128]{1,0:T(8,128)S(1)} %pad_maximum_fusion.small, f32[512,512]{1,0:T(8,128)} %vm_h.1, f32[512,512]{1,0:T(8,128)} %vt_h.1, ...), custom_call_target="tpu_custom_call" | custom-call | tf_op jit(solution)/shard_map/pallas_call | solution.py:639
  44.3 1.2 %shard_map.105 = (f32[3,8,16,512]{3,2,1,0:T(8,128)}, f32[3,8,16,512]{3,2,1,0:T(8,128)}) custom-call(f32[3,8,16,512]{3,2,1,0:T(8,128)S(1)} %get-tuple-element.4.next_ref, f32[3,8,16,512]{3,2,1,0:T(8,128)S(1)} %get-tuple-element.5.adj_ref), custom_call_target="tpu_custom_call" | custom-call | tf_op jit(solution)/shard_map/pallas_call | solution.py:687
  (1 shorter events, 0.0 us)
